TPU v7x, 32 devices: a whole 2x2x4 slice. The times are simulated.
32 devices in a mesh: grp: 2 (over y), date: 4 (over z), row: 4 (over x, core).
Axes of the slice: x: 2, y: 2, z: 4, core: 2. Of those that a mesh axis runs over, the one named last changes fastest.
Arguments:
- stack_data: float32 [16, 2, 64, 512], P(('grp', 'date'), None, 'row'), parts along dimension 0, may hold values from -40 to 40, as said below
- plan: int32 [8], replicated, may hold values from 0 to 7, each once
Outputs:
- coherence: float32 [16, 8, 2, 64, 512], P(('grp', 'date'), None, None, 'row'), parts along dimension 0
There are 2 independent parts, one for each index of `grp`. A program takes and returns all parts, laid end to end along the dimension named above; an argument that names none is the same for every part. Nothing has to cross between parts.
Inputs may be any that keep to these rules, and one draw needn't show every extreme that they name: `stack_data`: complex samples of one scene seen on every date, each date with its own phase, strength and noise.
All inputs are finite; a program needn't handle non-finite values.
Results may differ from a plain program's by a relative error of at most 0.00005.
Values sent between devices are 32-bit elements; how exact they have to be, the bound alone decides.
No kernel may reach another device: no remote copies, remote signals or barrier semaphores. Data moves between devices by JAX's collectives and lax.ppermute only.
A program may use at most 64 MiB of HBM per device.

v0:
```python
import jax
import jax.numpy as jnp
from jax import lax
from jax.sharding import PartitionSpec as P

HALF_ROWS = 4
HALF_COLS = 16


HIGH = lax.Precision.HIGHEST
epsilon = 1e-06


def extended(array, sides, width):
    for axis, dim in sides:
        size, length = (lax.axis_size(axis), array.shape[dim])
        up = [(i, (i + 1) % size) for i in range(size - 1)]
        down = [(j, i) for i, j in up]
        last = lax.slice_in_dim(array, length - width, length, axis=dim)
        first = lax.slice_in_dim(array, 0, width, axis=dim)
        before = lax.ppermute(last, axis, up)
        after = lax.ppermute(first, axis, down)
        array = jnp.concatenate([before, array, after], axis=dim)
    return array


def body(stack_data, plan):
    rows_dev = stack_data.shape[2]
    columns = stack_data.shape[3]
    haloed = extended(stack_data, (("row", 2),), HALF_ROWS)
    row_out = lax.broadcasted_iota(jnp.int32, (rows_dev, rows_dev + 2 * HALF_ROWS), 0)
    row_in = lax.broadcasted_iota(jnp.int32, (rows_dev, rows_dev + 2 * HALF_ROWS), 1)
    row_band = ((row_in >= row_out) & (row_in <= row_out + 2 * HALF_ROWS)).astype(jnp.float32)
    col_out = lax.broadcasted_iota(jnp.int32, (columns, columns), 0)
    col_in = lax.broadcasted_iota(jnp.int32, (columns, columns), 1)
    col_band = (jnp.abs(col_out - col_in) <= HALF_COLS).astype(jnp.float32)

    def window(field):
        summed = jnp.einsum("rs,...sc->...rc", row_band, field, precision=HIGH)
        return jnp.einsum("...rc,cd->...rd", summed, col_band, precision=HIGH)

    loc_real = haloed[:, 0]
    loc_imag = haloed[:, 1]
    loc_power = window(loc_real * loc_real + loc_imag * loc_imag)
    piece = lax.all_gather(haloed, "date", axis=0, tiled=True)
    oth_real = piece[:, 0]
    oth_imag = piece[:, 1]
    oth_power = window(oth_real * oth_real + oth_imag * oth_imag)
    cross_real = loc_real[:, None] * oth_real[None] + loc_imag[:, None] * oth_imag[None]
    cross_imag = loc_imag[:, None] * oth_real[None] - loc_real[:, None] * oth_imag[None]
    sums = window(jnp.stack([cross_real, cross_imag], axis=2))
    factor = 1.0 / jnp.sqrt(loc_power[:, None] * oth_power[None] + epsilon)
    in_order = sums * factor[:, :, None]
    coherence = jnp.take(in_order, plan, axis=1)
    return coherence


def solution(mesh):
    placed = (P(("grp", "date"), None, "row", None), P())
    return jax.shard_map(
        body,
        mesh=mesh,
        in_specs=placed,
        out_specs=P(("grp", "date"), None, None, "row", None),
        check_vma=False,
    )
```

profile of v0, /device:TPU:1, one launch (start us, length us, event | category | flops | bytes accessed | tf_op | source)
XLA Modules:
  0.0 34.2 jit_solution(6815068337701900033)
XLA Ops:
  0.0 0.9 %fusion.35 = (f32[2,2,4,512]{3,2,1,0:T(4,128)S(1)}, f32[2,2,4,512]{3,2,1,0:T(4,128)S(1)}) fusion(f32[2,2,16,512]{3,2,1,0:T(8,128)} %param.2), kind=kLoop, calls=%fused_computation.50 | loop fusion | bytes 131072 | tf_op jit(solution)/shard_map/slice | solution.py:19
  0.9 4.5 %collective-permute-start = (f32[2,2,4,512]{3,2,1,0:T(4,128)S(1)}, f32[2,2,4,512]{3,2,1,0:T(4,128)S(1)}, u32[]{:S(2)}, u32[]{:S(2)}) collective-permute-start(f32[2,2,4,512]{3,2,1,0:T(4,128)S(1)} %get-tuple-element.11), channel_id=1, source_target_pairs={{0,1},{1,2},{2,3},{4,5},{5,6},{6,7},{8,9},{9,10},{10,11},{12,13},{... | collective-permute-start | bytes 98312 | tf_op jit(solution)/shard_map/ppermute | solution.py:21
  5.4 1.9 %collective-permute-start.1 = (f32[2,2,4,512]{3,2,1,0:T(4,128)S(1)}, f32[2,2,4,512]{3,2,1,0:T(4,128)S(1)}, u32[]{:S(2)}, u32[]{:S(2)}) collective-permute-start(f32[2,2,4,512]{3,2,1,0:T(4,128)S(1)} %get-tuple-element.12), channel_id=1, source_target_pairs={{1,0},{2,1},{3,2},{5,4},{6,5},{7,6},{9,8},{10,9},{11,10},{13,12},{... | collective-permute-start | bytes 98312 | tf_op jit(solution)/shard_map/ppermute | solution.py:22
  7.3 0.7 %compare_and_fusion = pred[8]{0:T(512)(128)(4,1)S(1)} fusion(s32[8]{0:T(128)} %param.3), kind=kLoop, calls=%fused_computation.44 | loop fusion | flops 48 | bytes 40 | tf_op jit(solution)/shard_map/jit(_take)/and | solution.py:54
  8.0 0.7 %compare_select_fusion = s32[8]{0:T(128)S(1)} fusion(s32[8]{0:T(128)} %param.3), kind=kLoop, calls=%fused_computation.43 | loop fusion | flops 24 | bytes 64 | tf_op jit(solution)/shard_map/jit(_take)/jit(_where)/select_n | solution.py:54
  8.7 0.0 collective-permute-done
  8.7 2.0 %collective-permute-done.1 = f32[2,2,4,512]{3,2,1,0:T(4,128)S(1)} collective-permute-done((f32[2,2,4,512]{3,2,1,0:T(4,128)S(1)}, f32[2,2,4,512]{3,2,1,0:T(4,128)S(1)}, u32[]{:S(2)}, u32[]{:S(2)}) %collective-permute-start.1) | collective-permute-done | bytes 32800 | tf_op jit(solution)/shard_map/ppermute | solution.py:22
  10.6 0.9 %pad_maximum_fusion = f32[2,2,24,512]{3,2,1,0:T(8,128)S(1)} fusion(f32[2,2,4,512]{3,2,1,0:T(4,128)S(1)} %collective-permute-done.1, f32[2,2,16,512]{3,2,1,0:T(8,128)} %param.2, f32[2,2,4,512]{3,2,1,0:T(4,128)S(1)} %collective-permute-done), kind=kLoop, calls=%fused_computation.27 | loop fusion | flops 98304 | bytes 393216 | tf_op jit(solution)/shard_map/concatenate | solution.py:23
  11.6 17.2 %all_gather.3 = f32[8,2,24,512]{3,2,1,0:T(8,128)S(1)} all-gather(f32[2,2,24,512]{3,2,1,0:T(8,128)S(1)} %pad_maximum_fusion), channel_id=1, replica_groups=mesh['grp'=2,'date'=4,'row'=4] {'date'}, dimensions={0}, use_global_device_ids=true | all-gather | bytes 983040 | tf_op jit(solution)/shard_map/all_gather | solution.py:45
  28.8 0.2 convolution_bitcast_fusion.1
  29.0 0.3 convolution_bitcast_fusion
  29.3 0.1 slice_bitcast_fusion.1
  29.4 0.3 fusion.10
  29.7 0.4 %fusion.8 = f32[8,16,512]{2,1,0:T(8,128)S(1)} fusion(f32[8,16,512]{2,1,0:T(8,128)S(1)} %convolution_bitcast_fusion), kind=kOutput, calls=%fused_computation.12 | convolution fusion | flops 403439616 | bytes 524288 | tf_op jit(solution)/shard_map/...rc,cd->...rd/dot_general | solution.py:40
  30.2 0.1 add_rsqrt_fusion
  30.2 0.2 multiply_add_fusion
  30.5 0.8 %fusion.4 = f32[2,8,2,16,512]{4,3,2,1,0:T(8,128)S(1)} fusion(f32[2,8,1,24,512]{4,3,2,1,0:T(8,128)S(1)} %get-tuple-element.6, f32[2,8,1,24,512]{4,3,2,1,0:T(8,128)S(1)} %get-tuple-element.5, s32[16]{0:T(128)S(1)} %iota_add_fusion), kind=kOutput, calls=%fused_computation.5 | convolution fusion | flops 75891840 | bytes 2621504 | tf_op jit(solution)/shard_map/rs,...sc->...rc/dot_general | solution.py:39
  31.3 1.0 %convolution_multiply_fusion = f32[2,8,2,16,512]{4,3,2,1,0:T(8,128)S(1)} fusion(f32[2,8,2,16,512]{4,3,2,1,0:T(8,128)S(1)} %fusion.4, f32[2,8,16,512]{3,2,1,0:T(8,128)S(1)} %add_rsqrt_fusion), kind=kOutput, calls=%fused_computation.6 | convolution fusion | flops 1611661312 | bytes 2621440 | tf_op jit(solution)/shard_map/...rc,cd->...rd/dot_general | solution.py:40
  32.3 0.6 %gather_fusion = f32[8,2,2,16,512]{4,3,2,1,0:T(8,128)S(1)} fusion(f32[2,8,2,16,512]{4,3,2,1,0:T(8,128)S(1)} %convolution_multiply_fusion, s32[1024]{0:T(1024)S(1)} %pad_clamp_fusion), kind=kCustom, calls=%fused_computation | custom fusion | bytes 2097184 | tf_op jit(solution)/shard_map/jit(_take)/gather | solution.py:54
  32.9 0.2 select_bitcast_fusion
  33.1 1.1 %copy.8 = f32[2,8,2,16,512]{4,3,2,1,0:T(8,128)} copy(f32[2,8,2,16,512]{4,3,2,0,1:T(8,128)S(1)} %select_bitcast_fusion) | data formatting | bytes 2097152 | tf_op jit(solution)/shard_map/jit(_take)/select_n | solution.py:54
  (3 shorter events, 0.0 us)
Async XLA Ops:
  0.9 7.8 %collective-permute-start = (f32[2,2,4,512]{3,2,1,0:T(4,128)S(1)}, f32[2,2,4,512]{3,2,1,0:T(4,128)S(1)}, u32[]{:S(2)}, u32[]{:S(2)}) collective-permute-start(f32[2,2,4,512]{3,2,1,0:T(4,128)S(1)} %get-tuple-element.11), channel_id=1, source_target_pairs={{0,1},{1,2},{2,3},{4,5},{5,6},{6,7},{8,9},{9,10},{10,11},{12,13},{... | collective-permute-start | bytes 98312 | tf_op jit(solution)/shard_map/ppermute | solution.py:21
  5.4 5.2 %collective-permute-start.1 = (f32[2,2,4,512]{3,2,1,0:T(4,128)S(1)}, f32[2,2,4,512]{3,2,1,0:T(4,128)S(1)}, u32[]{:S(2)}, u32[]{:S(2)}) collective-permute-start(f32[2,2,4,512]{3,2,1,0:T(4,128)S(1)} %get-tuple-element.12), channel_id=1, source_target_pairs={{1,0},{2,1},{3,2},{5,4},{6,5},{7,6},{9,8},{10,9},{11,10},{13,12},{... | collective-permute-start | bytes 98312 | tf_op jit(solution)/shard_map/ppermute | solution.py:22
where the time goes:
time: 34.4 us; the launch traced here: 34.2 us
  blocking collectives  17.2 us (50%)
  starting transfers between devices  6.43 us (19%)
  matrix products  3.09 us (9%)
  other arithmetic  2.78 us (8%)
  local copies, waits for them, and re-layouts  2.65 us (8%)
  waiting for transfers between devices  1.96 us (6%)
    all_gather x1, blocking collectives, body(): piece = lax.all_gather(haloed, 'date', axis=0, tiled=True)  17.2 us
    ppermute x1, starting transfers between devices, extended(): before = lax.ppermute(last, axis, up)  4.51 us
    ppermute x1, waiting for transfers between devices, extended(): after = lax.ppermute(first, axis, down)  1.96 us
    ppermute x1, starting transfers between devices, extended(): after = lax.ppermute(first, axis, down)  1.92 us
    dot_general x3, matrix products, window(): return jnp.einsum('...rc,cd->...rd', summed, col_band, precision=HIGH)  1.74 us
    dot_general x3, matrix products, window(): summed = jnp.einsum('rs,...sc->...rc', row_band, field, precision=HIGH)  1.35 us
    select_n x1, local copies, waits for them, and re-layouts, body(): coherence = jnp.take(in_order, plan, axis=1)  1.08 us
    concatenate x1, other arithmetic, extended(): array = jnp.concatenate([before, array, after], axis=dim)  0.94 us
  transfers between devices with their start and end apart: 2, of which 1 were waited for; matrix products, arithmetic and copies ran while one was open for 4% of the time, Pallas kernels for 0%

commit v1 on v0

v1 whole, which is shorter than its diff:
```python
import functools

import jax
import jax.numpy as jnp
from jax import lax
from jax.experimental import pallas as pl
from jax.experimental.pallas import tpu as pltpu
from jax.sharding import PartitionSpec as P

HALF_ROWS = 4
HALF_COLS = 16
epsilon = 1e-06


def split(x):
    high = x.astype(jnp.bfloat16)
    low = (x - high.astype(jnp.float32)).astype(jnp.bfloat16)
    return high, low


def row_window(f, rows):
    length = f.shape[0]
    total, width = f, 1
    while width < 2 * HALF_ROWS:
        total = total + pltpu.roll(total, length - width, 0)
        width *= 2
    return total[:rows] + f[2 * HALF_ROWS:]


def kernel(n_parts, nd, direct, plan_ref, own_ref, own_a, own_b, *rest):
    parts = rest[:n_parts]
    rim_a = rest[n_parts:2 * n_parts]
    rim_b = rest[2 * n_parts:3 * n_parts]
    band_ref, out_ref, ext, res, buf, where, sems = rest[3 * n_parts:]
    rows, cols = own_ref.shape[2], own_ref.shape[3]
    per_part = parts[0].shape[0]
    slots = n_parts * per_part
    n_dates = plan_ref.shape[0]
    me = lax.axis_index("date")
    odd = lax.axis_index("row") % 2 == 1
    step = pl.program_id(0)

    def place(k, _):
        j = plan_ref[k]
        if direct:
            slot = ((j // nd) ^ me) * nd + j % nd
        else:
            slot = j
        where[slot] = k
        return 0

    @pl.when(step == 0)
    def _():
        lax.fori_loop(0, n_dates, place, 0)

    def fill(dst, block, ra, rb):
        a, b = ra[...], rb[...]
        ext[dst, :, :HALF_ROWS] = jnp.where(odd, a, b)
        ext[dst, :, HALF_ROWS:HALF_ROWS + rows] = block[...]
        ext[dst, :, HALF_ROWS + rows:] = jnp.where(odd, b, a)

    band = band_ref[...]

    def columns(fields):
        high, low = zip(*(split(f) for f in fields))
        both = jnp.concatenate(high + low, axis=0)
        out = jnp.dot(both, band, preferred_element_type=jnp.float32)
        half = out.shape[0] // 2
        return out[:half] + out[half:]

    mine = slice(slots, slots + nd)
    for d in range(nd):
        fill(slots + d, own_ref.at[d], own_a.at[d], own_b.at[d])
    for p in range(n_parts):
        for d in range(per_part):
            fill(p * per_part + d, parts[p].at[d], rim_a[p].at[d], rim_b[p].at[d])

    own_fields = []
    for d in range(nd):
        re, im = ext[slots + d, 0], ext[slots + d, 1]
        own_fields.append(row_window(re * re + im * im, rows))
    own_power = columns(own_fields)
    copies = []
    for s in range(slots):
        re, im = ext[s, 0], ext[s, 1]
        fields = [row_window(re * re + im * im, rows)]
        for d in range(nd):
            mr, mi = ext[slots + d, 0], ext[slots + d, 1]
            fields.append(row_window(mr * re + mi * im, rows))
            fields.append(row_window(mi * re - mr * im, rows))
        res[s] = columns(fields)
        power = res[s, :rows]
        k = where[step * slots + s]
        for d in range(nd):
            factor = lax.rsqrt(own_power[d * rows:(d + 1) * rows] * power + epsilon)
            at = (1 + 2 * d) * rows
            buf[s, d, 0] = res[s, at:at + rows] * factor
            buf[s, d, 1] = res[s, at + rows:at + 2 * rows] * factor
            copy = pltpu.make_async_copy(buf.at[s, d], out_ref.at[d, k], sems.at[s, d])
            copy.start()
            copies.append(copy)
    for copy in copies:
        copy.wait()


def pairs_of(size, flip):
    return [(i, i ^ flip) for i in range(size) if (i ^ flip) < size]


def body(stack_data, plan):
    nd, _, rows, cols = stack_data.shape
    size, n_rows = lax.axis_size("date"), lax.axis_size("row")
    direct = size in (2, 4)
    odd = lax.axis_index("row") % 2

    inner = pairs_of(n_rows, 1)
    outer = [(i, i + 1) for i in range(1, n_rows - 1, 2)]
    outer = outer + [(j, i) for i, j in outer]

    def rims(blocks):
        last = [b[:, :, rows - HALF_ROWS:] for b in blocks]
        first = [b[:, :, :HALF_ROWS] for b in blocks]
        last, first = (jnp.concatenate(x, axis=0) for x in (last, first))
        a = lax.ppermute(jnp.where(odd == 1, first, last), "row", inner)
        b = lax.ppermute(jnp.where(odd == 1, last, first), "row", outer)
        return a, b

    if direct:
        parts = [stack_data] + [
            lax.ppermute(stack_data, "date", pairs_of(size, m)) for m in range(1, size)
        ]
        a, b = rims(parts)
        n_parts, per_part, grid = size, nd, 1
        rim_a = [a[m * nd:(m + 1) * nd] for m in range(size)]
        rim_b = [b[m * nd:(m + 1) * nd] for m in range(size)]
        own_a, own_b = rim_a[0], rim_b[0]
    else:
        gathered = lax.all_gather(stack_data, "date", axis=0, tiled=True)
        a, b = rims([gathered, stack_data])
        n_parts, per_part = 1, 8 if (size * nd) % 8 == 0 else nd
        grid = size * nd // per_part
        parts, rim_a, rim_b = [gathered], [a[:size * nd]], [b[:size * nd]]
        own_a, own_b = a[size * nd:], b[size * nd:]

    out_col = lax.broadcasted_iota(jnp.int32, (cols, cols), 0)
    in_col = lax.broadcasted_iota(jnp.int32, (cols, cols), 1)
    band = (jnp.abs(out_col - in_col) <= HALF_COLS).astype(jnp.bfloat16)

    slots = n_parts * per_part

    def whole(shape):
        return pl.BlockSpec(shape, lambda g: (0,) * len(shape))

    def chunk(shape):
        return pl.BlockSpec(shape, lambda g: (g, 0, 0, 0))

    rim_shape = (HALF_ROWS, cols)
    return pl.pallas_call(
        functools.partial(kernel, n_parts, nd, direct),
        grid=(grid,),
        out_shape=jax.ShapeDtypeStruct((nd, size * nd, 2, rows, cols), jnp.float32),
        in_specs=[
            pl.BlockSpec(memory_space=pltpu.SMEM),
            whole((nd, 2, rows, cols)),
            whole((nd, 2) + rim_shape),
            whole((nd, 2) + rim_shape),
        ]
        + [chunk((per_part, 2, rows, cols))] * n_parts
        + [chunk((per_part, 2) + rim_shape)] * (2 * n_parts)
        + [whole((cols, cols))],
        out_specs=pl.BlockSpec(memory_space=pl.ANY),
        scratch_shapes=[
            pltpu.VMEM((slots + nd, 2, rows + 2 * HALF_ROWS, cols), jnp.float32),
            pltpu.VMEM((slots, (1 + 2 * nd) * rows, cols), jnp.float32),
            pltpu.VMEM((slots, nd, 2, rows, cols), jnp.float32),
            pltpu.SMEM((size * nd,), jnp.int32),
            pltpu.SemaphoreType.DMA((slots, nd)),
        ],
        compiler_params=pltpu.CompilerParams(vmem_limit_bytes=32 * 2**20),
        name="coherence",
    )(plan, stack_data, own_a, own_b, *parts, *rim_a, *rim_b, band)


def solution(mesh):
    placed = (P(("grp", "date"), None, "row", None), P())
    return jax.shard_map(
        body,
        mesh=mesh,
        in_specs=placed,
        out_specs=P(("grp", "date"), None, None, "row", None),
        check_vma=False,
    )
```

time: 34.4 us -> 25.5 us (0.74)
  the two profiles are of different devices: /device:TPU:1 before, /device:TPU:17 now
where the time goes in v1:
time: 25.5 us; the launch traced here: 25.3 us
  waiting for transfers between devices  14 us (55%)
  starting transfers between devices  6.22 us (24%)
  Pallas kernels  3.04 us (12%)
  local copies, waits for them, and re-layouts  1.81 us (7%)
    ppermute x3, waiting for transfers between devices, body(): lax.ppermute(stack_data, 'date', pairs_of(size, m))  11.4 us
    ppermute x1, starting transfers between devices, rims(): b = lax.ppermute(jnp.where(odd == 1, last, first), 'row', outer)  3.5 us
    pallas_call x1, Pallas kernels, body(): pl.pallas_call(functools.partial(kernel, n_parts, nd, direct), grid=(grid...  3.04 us
    ppermute x3, starting transfers between devices, body(): lax.ppermute(stack_data, 'date', pairs_of(size, m))  2.65 us
    ppermute x1, waiting for transfers between devices, rims(): b = lax.ppermute(jnp.where(odd == 1, last, first), 'row', outer)  2.62 us
    slice x4, local copies, waits for them, and re-layouts, rims(): first = [b[:, :, :HALF_ROWS] for b in blocks]  0.93 us
    unnamed x4, local copies, waits for them, and re-layouts  0.86 us
  transfers between devices with their start and end apart: 5, of which 4 were waited for; matrix products, arithmetic and copies ran while one was open for 4% of the time, Pallas kernels for 0%

profile of v1, /device:TPU:17, one launch (start us, length us, event | category | flops | bytes accessed | tf_op | source)
XLA Modules:
  0.0 25.3 jit_solution(1635197272645050335)
XLA Ops:
  0.0 0.0 collective-permute-start.1
  0.0 1.3 %collective-permute-start = (f32[2,2,16,512]{3,2,1,0:T(8,128)}, f32[2,2,16,512]{3,2,1,0:T(8,128)S(1)}, u32[]{:S(2)}, u32[]{:S(2)}) collective-permute-start(f32[2,2,16,512]{3,2,1,0:T(8,128)} %rest_0_.1), channel_id=1, source_target_pairs={{0,4},{4,0},{8,12},{12,8},{1,5},{5,1},{9,13},{13,9},{2,6},{6,2},{1... | collective-permute-start | bytes 393224 | tf_op jit(solution)/shard_map/ppermute | solution.py:130
  1.4 1.3 %collective-permute-start.2 = (f32[2,2,16,512]{3,2,1,0:T(8,128)}, f32[2,2,16,512]{3,2,1,0:T(8,128)S(1)}, u32[]{:S(2)}, u32[]{:S(2)}) collective-permute-start(f32[2,2,16,512]{3,2,1,0:T(8,128)} %rest_0_.1), channel_id=1, source_target_pairs={{0,12},{4,8},{8,4},{12,0},{1,13},{5,9},{9,5},{13,1},{2,14},{6,10},... | collective-permute-start | bytes 393224 | tf_op jit(solution)/shard_map/ppermute | solution.py:130
  2.6 0.9 %fusion.3 = (f32[2,2,4,512]{3,2,1,0:T(4,128)S(1)}, f32[2,2,4,512]{3,2,1,0:T(4,128)S(1)}) fusion(f32[2,2,16,512]{3,2,1,0:T(8,128)} %rest_0_.1), kind=kLoop, calls=%fused_computation.8 | loop fusion | bytes 131072 | tf_op jit(solution)/shard_map/slice | solution.py:122
  3.5 1.9 %collective-permute-done.1.rest_2_ = f32[2,2,16,512]{3,2,1,0:T(8,128)S(1)} collective-permute-done((f32[2,2,16,512]{3,2,1,0:T(8,128)}, f32[2,2,16,512]{3,2,1,0:T(8,128)S(1)}, u32[]{:S(2)}, u32[]{:S(2)}) %collective-permute-start.1) | collective-permute-done | bytes 131104 | tf_op jit(solution)/shard_map/ppermute | solution.py:130
  5.5 1.9 %collective-permute-done.rest_1_ = f32[2,2,16,512]{3,2,1,0:T(8,128)S(1)} collective-permute-done((f32[2,2,16,512]{3,2,1,0:T(8,128)}, f32[2,2,16,512]{3,2,1,0:T(8,128)S(1)}, u32[]{:S(2)}, u32[]{:S(2)}) %collective-permute-start) | collective-permute-done | bytes 131104 | tf_op jit(solution)/shard_map/ppermute | solution.py:130
  7.4 7.6 %collective-permute-done.2.rest_3_ = f32[2,2,16,512]{3,2,1,0:T(8,128)S(1)} collective-permute-done((f32[2,2,16,512]{3,2,1,0:T(8,128)}, f32[2,2,16,512]{3,2,1,0:T(8,128)S(1)}, u32[]{:S(2)}, u32[]{:S(2)}) %collective-permute-start.2) | collective-permute-done | bytes 131104 | tf_op jit(solution)/shard_map/ppermute | solution.py:130
  15.0 0.1 broadcast_select_fusion
  15.1 3.5 %collective-permute-start.4 = (f32[8,2,4,512]{3,2,1,0:T(4,128)S(1)}, f32[8,2,4,512]{3,2,1,0:T(4,128)S(1)}, u32[]{:S(2)}, u32[]{:S(2)}) collective-permute-start(f32[8,2,4,512]{3,2,1,0:T(4,128)S(1)} %get-tuple-element.5), channel_id=1, source_target_pairs={{1,2},{2,1},{5,6},{6,5},{9,10},{10,9},{13,14},{14,13},{17,18},{18,... | collective-permute-start | bytes 393224 | tf_op jit(solution)/shard_map/ppermute | solution.py:125
  18.6 0.1 fusion.rest_12_
  18.6 0.1 collective-permute-start.3
  18.7 2.6 %collective-permute-done.4 = f32[8,2,4,512]{3,2,1,0:T(4,128)S(1)} collective-permute-done((f32[8,2,4,512]{3,2,1,0:T(4,128)S(1)}, f32[8,2,4,512]{3,2,1,0:T(4,128)S(1)}, u32[]{:S(2)}, u32[]{:S(2)}) %collective-permute-start.4) | collective-permute-done | bytes 131104 | tf_op jit(solution)/shard_map/ppermute | solution.py:125
  21.4 0.0 copy-start
  21.4 0.0 collective-permute-done.3
  21.4 0.0 copy-start.1
  21.4 0.9 %copy-done = f32[2,2,16,512]{3,2,1,0:T(8,128)S(1)} copy-done((f32[2,2,16,512]{3,2,1,0:T(8,128)S(1)}, f32[2,2,16,512]{3,2,1,0:T(8,128)}, u32[]{:S(2)}) %copy-start) | copy-done | bytes 131096
  22.3 0.0 copy-done.1
  22.3 3.0 %coherence.1 = f32[2,8,2,16,512]{4,3,2,1,0:T(8,128)} custom-call(s32[8]{0:T(128)S(1)} %copy-done.1, f32[2,2,16,512]{3,2,1,0:T(8,128)S(1)} %copy-done, f32[2,2,4,512]{3,2,1,0:T(4,128)S(1)} %get-tuple-element.14.own_a.rest_4_, f32[2,2,4,512]{3,2,1,0:T(4,128)S(1)} %get-tuple-element.10.own_b.rest_8_, f32[2,2,16,512]{3,2,1,0:T(8,128)S(1)} %copy-done, ...), custom_call_target="tpu_custom_call" | custom-call | tf_op jit(solution)/shard_map/coherence/pallas_call | solution.py:158
  (5 shorter events, 0.1 us)
Async XLA Ops:
  0.0 5.5 %collective-permute-start.1 = (f32[2,2,16,512]{3,2,1,0:T(8,128)}, f32[2,2,16,512]{3,2,1,0:T(8,128)S(1)}, u32[]{:S(2)}, u32[]{:S(2)}) collective-permute-start(f32[2,2,16,512]{3,2,1,0:T(8,128)} %rest_0_.1), channel_id=1, source_target_pairs={{0,8},{4,12},{8,0},{12,4},{1,9},{5,13},{9,1},{13,5},{2,10},{6,14},... | collective-permute-start | bytes 393224 | tf_op jit(solution)/shard_map/ppermute | solution.py:130
  0.0 7.4 %collective-permute-start = (f32[2,2,16,512]{3,2,1,0:T(8,128)}, f32[2,2,16,512]{3,2,1,0:T(8,128)S(1)}, u32[]{:S(2)}, u32[]{:S(2)}) collective-permute-start(f32[2,2,16,512]{3,2,1,0:T(8,128)} %rest_0_.1), channel_id=1, source_target_pairs={{0,4},{4,0},{8,12},{12,8},{1,5},{5,1},{9,13},{13,9},{2,6},{6,2},{1... | collective-permute-start | bytes 393224 | tf_op jit(solution)/shard_map/ppermute | solution.py:130
  1.4 13.6 %collective-permute-start.2 = (f32[2,2,16,512]{3,2,1,0:T(8,128)}, f32[2,2,16,512]{3,2,1,0:T(8,128)S(1)}, u32[]{:S(2)}, u32[]{:S(2)}) collective-permute-start(f32[2,2,16,512]{3,2,1,0:T(8,128)} %rest_0_.1), channel_id=1, source_target_pairs={{0,12},{4,8},{8,4},{12,0},{1,13},{5,9},{9,5},{13,1},{2,14},{6,10},... | collective-permute-start | bytes 393224 | tf_op jit(solution)/shard_map/ppermute | solution.py:130
  15.1 6.3 %collective-permute-start.4 = (f32[8,2,4,512]{3,2,1,0:T(4,128)S(1)}, f32[8,2,4,512]{3,2,1,0:T(4,128)S(1)}, u32[]{:S(2)}, u32[]{:S(2)}) collective-permute-start(f32[8,2,4,512]{3,2,1,0:T(4,128)S(1)} %get-tuple-element.5), channel_id=1, source_target_pairs={{1,2},{2,1},{5,6},{6,5},{9,10},{10,9},{13,14},{14,13},{17,18},{18,... | collective-permute-start | bytes 393224 | tf_op jit(solution)/shard_map/ppermute | solution.py:125
  18.6 2.7 %collective-permute-start.3 = (f32[8,2,4,512]{3,2,1,0:T(4,128)S(1)}, f32[8,2,4,512]{3,2,1,0:T(4,128)S(1)}, u32[]{:S(2)}, u32[]{:S(2)}) collective-permute-start(f32[8,2,4,512]{3,2,1,0:T(4,128)S(1)} %get-tuple-element.6), channel_id=1, source_target_pairs={{0,1},{1,0},{2,3},{3,2},{4,5},{5,4},{6,7},{7,6},{8,9},{9,8},{10,11... | collective-permute-start | bytes 393224 | tf_op jit(solution)/shard_map/ppermute | solution.py:124
  21.4 0.9 %copy-start = (f32[2,2,16,512]{3,2,1,0:T(8,128)S(1)}, f32[2,2,16,512]{3,2,1,0:T(8,128)}, u32[]{:S(2)}) copy-start(f32[2,2,16,512]{3,2,1,0:T(8,128)} %rest_0_.1) | copy-start | bytes 393220
  21.4 0.9 %copy-start.1 = (s32[8]{0:T(128)S(1)}, s32[8]{0:T(128)}, u32[]{:S(2)}) copy-start(s32[8]{0:T(128)} %plan_ref.1) | copy-start | bytes 100

commit v2 on v1

v2 whole, which is shorter than its diff:
```python
import functools

import jax
import jax.numpy as jnp
from jax import lax
from jax.experimental import pallas as pl
from jax.experimental.pallas import tpu as pltpu
from jax.sharding import PartitionSpec as P

HALF_ROWS = 4
HALF_COLS = 16
epsilon = 1e-06


def split(x):
    high = x.astype(jnp.bfloat16)
    low = (x - high.astype(jnp.float32)).astype(jnp.bfloat16)
    return high, low


def row_window(f, rows):
    length = f.shape[0]
    total, width = f, 1
    while width < 2 * HALF_ROWS:
        total = total + pltpu.roll(total, length - width, 0)
        width *= 2
    return total[:rows] + f[2 * HALF_ROWS:]


def kernel(counts, nd, direct, n_rows, plan_ref, *refs):
    n_blocks, n_rims = len(counts[0]), len(counts[1])
    edges, refs = refs[:n_blocks], refs[n_blocks:]
    inners, refs = refs[:n_blocks], refs[n_blocks:]
    rim_c, refs = refs[:n_rims], refs[n_rims:]
    rim_x, refs = refs[:n_rims], refs[n_rims:]
    band_ref, out_ref, ext, res, buf, where, sems = refs
    half = HALF_ROWS
    rows, cols = inners[0].shape[2] + 2 * half, inners[0].shape[3]
    total = sum(counts[0])
    first = 0 if direct else nd
    slots = total - first
    row = lax.axis_index("row")
    me = lax.axis_index("date")
    odd = row % 2 == 1
    step = 0 if direct else pl.program_id(0)

    def place(k, _):
        j = plan_ref[k]
        where[((j // nd) ^ me) * nd + j % nd if direct else j] = k
        return 0

    if direct:
        lax.fori_loop(0, plan_ref.shape[0], place, 0)
    else:

        @pl.when(step == 0)
        def _():
            lax.fori_loop(0, plan_ref.shape[0], place, 0)

    at = 0
    for ref, inner, count in zip(edges, inners, counts[0]):
        for d in range(count):
            ext[at, :, half:2 * half] = ref[d, :, half:]
            ext[at, :, 2 * half:rows] = inner[d]
            ext[at, :, rows:rows + half] = ref[d, :, :half]
            at += 1
    at = 0
    for c, x, count in zip(rim_c, rim_x, counts[1]):
        for d in range(count):
            top = jnp.where(odd, c[d], x[d])
            bottom = jnp.where(odd, x[d], c[d])
            ext[at, :, :half] = jnp.where(row == 0, 0.0, top)
            ext[at, :, rows + half:] = jnp.where(row == n_rows - 1, 0.0, bottom)
            at += 1

    band = band_ref[...]

    def columns(fields):
        high, low = zip(*(split(f) for f in fields))
        both = jnp.concatenate(high + low, axis=0)
        out = jnp.dot(both, band, preferred_element_type=jnp.float32)
        middle = out.shape[0] // 2
        return out[:middle] + out[middle:]

    own_fields = []
    for d in range(nd):
        re, im = ext[d, 0], ext[d, 1]
        own_fields.append(row_window(re * re + im * im, rows))
    own_power = columns(own_fields)
    copies = []
    for s in range(slots):
        re, im = ext[first + s, 0], ext[first + s, 1]
        fields = [row_window(re * re + im * im, rows)]
        for d in range(nd):
            mr, mi = ext[d, 0], ext[d, 1]
            fields.append(row_window(mr * re + mi * im, rows))
            fields.append(row_window(mi * re - mr * im, rows))
        res[s] = columns(fields)
        power = res[s, :rows]
        k = where[step * slots + s]
        for d in range(nd):
            factor = lax.rsqrt(own_power[d * rows:(d + 1) * rows] * power + epsilon)
            at = (1 + 2 * d) * rows
            buf[s, d, 0] = res[s, at:at + rows] * factor
            buf[s, d, 1] = res[s, at + rows:at + 2 * rows] * factor
            copy = pltpu.make_async_copy(buf.at[s, d], out_ref.at[d, k], sems.at[s, d])
            copy.start()
            copies.append(copy)
    for copy in copies:
        copy.wait()


def pairs_of(size, flip):
    return [(i, i ^ flip) for i in range(size)]


def body(stack_data, plan):
    nd, _, rows, cols = stack_data.shape
    size, n_rows = lax.axis_size("date"), lax.axis_size("row")
    half = HALF_ROWS
    direct = size == 4
    odd = lax.axis_index("row") % 2 == 1

    near = [(i, i ^ 1) for i in range(n_rows) if (i ^ 1) < n_rows]
    far = [(i, (i + 1) % n_rows) for i in range(1, n_rows, 2)] if n_rows % 2 == 0 else [
        (i, i + 1) for i in range(1, n_rows - 1, 2)]
    far = far + [(j, i) for i, j in far if i != j]

    def cut(block):
        first, last = block[:, :, :half], block[:, :, rows - half:]
        return jnp.concatenate([last, first], axis=2), block[:, :, half:rows - half]

    def rims(edge):
        last, first = edge[:, :, :half], edge[:, :, half:]
        c = lax.ppermute(jnp.where(odd, first, last), "row", near)
        x = lax.ppermute(jnp.where(odd, last, first), "row", far)
        return c, x

    edge, inner = cut(stack_data)
    if direct:
        edge_2 = lax.ppermute(edge, "date", pairs_of(size, 2))
        edge_1 = lax.ppermute(edge, "date", pairs_of(size, 1))
        inner_2 = lax.ppermute(inner, "date", pairs_of(size, 2))
        inner_1 = lax.ppermute(inner, "date", pairs_of(size, 1))
        edge_3 = lax.ppermute(edge_2, "date", pairs_of(size, 1))
        rims_a = rims(jnp.concatenate([edge, edge_1, edge_2], axis=0))
        inner_3 = lax.ppermute(inner_2, "date", pairs_of(size, 1))
        rims_b = rims(edge_3)
        edges, inners = [edge, edge_1, edge_2, edge_3], [inner, inner_1, inner_2, inner_3]
        rim_c, rim_x = [rims_a[0], rims_b[0]], [rims_a[1], rims_b[1]]
        chunked = [False] * 4, [False] * 2
        grid, slots = None, size * nd
    else:
        gathered = lax.all_gather(stack_data, "date", axis=0, tiled=True)
        all_edge, all_inner = cut(gathered)
        rim_own, rim_all = rims(edge), rims(all_edge)
        edges, inners = [edge, all_edge], [inner, all_inner]
        rim_c, rim_x = [rim_own[0], rim_all[0]], [rim_own[1], rim_all[1]]
        chunked = [False, True], [False, True]
        slots = 8 if (size * nd) % 8 == 0 else nd
        grid = (size * nd // slots,)

    out_col = lax.broadcasted_iota(jnp.int32, (cols, cols), 0)
    in_col = lax.broadcasted_iota(jnp.int32, (cols, cols), 1)
    band = (jnp.abs(out_col - in_col) <= HALF_COLS).astype(jnp.bfloat16)

    def spec(array, chunk=False):
        if grid is None:
            return pl.BlockSpec(memory_space=pltpu.VMEM)
        if chunk:
            return pl.BlockSpec((slots,) + array.shape[1:], lambda g: (g, 0, 0, 0))
        return pl.BlockSpec(array.shape, lambda g: (0,) * array.ndim)

    def count(arrays, chunks):
        return [slots if c else a.shape[0] for a, c in zip(arrays, chunks)]

    counts = count(edges, chunked[0]), count(rim_c, chunked[1])
    total = sum(counts[0])
    operands = edges + inners + rim_c + rim_x
    chunks = chunked[0] * 2 + chunked[1] * 2
    return pl.pallas_call(
        functools.partial(kernel, counts, nd, direct, n_rows),
        **({} if grid is None else {"grid": grid}),
        out_shape=jax.ShapeDtypeStruct((nd, size * nd, 2, rows, cols), jnp.float32),
        in_specs=[pl.BlockSpec(memory_space=pltpu.SMEM)]
        + [spec(a, c) for a, c in zip(operands, chunks)]
        + [spec(band)],
        out_specs=pl.BlockSpec(memory_space=pl.ANY),
        scratch_shapes=[
            pltpu.VMEM((total, 2, rows + 2 * half, cols), jnp.float32),
            pltpu.VMEM((slots, (1 + 2 * nd) * rows, cols), jnp.float32),
            pltpu.VMEM((slots, nd, 2, rows, cols), jnp.float32),
            pltpu.SMEM((size * nd,), jnp.int32),
            pltpu.SemaphoreType.DMA((slots, nd)),
        ],
        compiler_params=pltpu.CompilerParams(vmem_limit_bytes=32 * 2**20),
        name="coherence",
    )(plan, *operands, band)


def solution(mesh):
    placed = (P(("grp", "date"), None, "row", None), P())
    return jax.shard_map(
        body,
        mesh=mesh,
        in_specs=placed,
        out_specs=P(("grp", "date"), None, None, "row", None),
        check_vma=False,
    )
```

time: 25.5 us -> 20.4 us (0.80)
  the two profiles are of different devices: /device:TPU:17 before, /device:TPU:0 now
where the time goes in v2:
time: 20.4 us; the launch traced here: 20.2 us
  starting transfers between devices  12.5 us (61%)
  waiting for transfers between devices  3.56 us (17%)
  Pallas kernels  2.94 us (14%)
  local copies, waits for them, and re-layouts  0.94 us (5%)
    ppermute x1, starting transfers between devices, body(): edge_2 = lax.ppermute(edge, 'date', pairs_of(size, 2))  4.1 us
    pallas_call x1, Pallas kernels, body(): pl.pallas_call(functools.partial(kernel, counts, nd, direct, n_rows), **{...  2.94 us
    ppermute x2, starting transfers between devices, rims(): c = lax.ppermute(jnp.where(odd, first, last), 'row', near)  2.91 us
    ppermute x1, starting transfers between devices, body(): edge_3 = lax.ppermute(edge_2, 'date', pairs_of(size, 1))  2.05 us
    ppermute x1, starting transfers between devices, body(): edge_1 = lax.ppermute(edge, 'date', pairs_of(size, 1))  1.58 us
    ppermute x1, waiting for transfers between devices, body(): inner_3 = lax.ppermute(inner_2, 'date', pairs_of(size, 1))  1.47 us
    slice x1, local copies, waits for them, and re-layouts, cut(): first, last = (block[:, :, :half], block[:, :, rows - half:])  0.93 us
    ppermute x1, starting transfers between devices, body(): inner_3 = lax.ppermute(inner_2, 'date', pairs_of(size, 1))  0.89 us
  transfers between devices with their start and end apart: 10, of which 6 were waited for; matrix products, arithmetic and copies ran while one was open for 1% of the time, Pallas kernels for 0%

profile of v2, /device:TPU:0, one launch (start us, length us, event | category | flops | bytes accessed | tf_op | source)
XLA Modules:
  0.0 20.2 jit_solution(11956265593259872104)
XLA Ops:
  0.0 0.0 copy-start.1
  0.0 0.9 %fusion.1 = (f32[2,2,4,512]{3,2,1,0:T(4,128)S(1)}, f32[2,2,4,512]{3,2,1,0:T(4,128)S(1)}) fusion(f32[2,2,16,512]{3,2,1,0:T(8,128)} %param.2), kind=kLoop, calls=%fused_computation.8 | loop fusion | bytes 131072 | tf_op jit(solution)/shard_map/slice | solution.py:130
  1.0 4.1 %collective-permute-start.1 = (f32[2,2,8,512]{3,2,1,0:T(8,128)S(1)}, f32[2,2,8,512]{3,2,1,0:T(8,128)S(1)}, u32[]{:S(2)}, u32[]{:S(2)}) collective-permute-start(f32[2,2,8,512]{3,2,1,0:T(8,128)S(1)} %pad_maximum_fusion.1.refs_0_), channel_id=1, source_target_pairs={{0,8},{4,12},{8,0},{12,4},{1,9},{5,13},{9,1},{13,5},{2,10},{6,14},... | collective-permute-start | bytes 196616 | tf_op jit(solution)/shard_map/ppermute | solution.py:141
  5.1 1.6 %collective-permute-start = (f32[2,2,8,512]{3,2,1,0:T(8,128)S(1)}, f32[2,2,8,512]{3,2,1,0:T(8,128)S(1)}, u32[]{:S(2)}, u32[]{:S(2)}) collective-permute-start(f32[2,2,8,512]{3,2,1,0:T(8,128)S(1)} %pad_maximum_fusion.1.refs_0_), channel_id=1, source_target_pairs={{0,4},{4,0},{8,12},{12,8},{1,5},{5,1},{9,13},{13,9},{2,6},{6,2},{1... | collective-permute-start | bytes 196616 | tf_op jit(solution)/shard_map/ppermute | solution.py:142
  6.6 0.0 copy-done.1
  6.7 0.4 %collective-permute-start.4 = (f32[2,2,8,512]{3,2,1,0:T(8,128)S(1)}, f32[2,2,8,512]{3,2,1,0:T(8,128)S(1)}, u32[]{:S(2)}, u32[]{:S(2)}) collective-permute-start(f32[2,2,8,512]{3,2,1,0:T(8,128)S(1)} %slice.23.refs_4_), channel_id=1, source_target_pairs={{0,8},{4,12},{8,0},{12,4},{1,9},{5,13},{9,1},{13,5},{2,10},{6,14},... | collective-permute-start | bytes 196616 | tf_op jit(solution)/shard_map/ppermute | solution.py:143
  7.1 0.2 collective-permute-start.3
  7.2 0.9 %collective-permute-done.1.refs_2_ = f32[2,2,8,512]{3,2,1,0:T(8,128)S(1)} collective-permute-done((f32[2,2,8,512]{3,2,1,0:T(8,128)S(1)}, f32[2,2,8,512]{3,2,1,0:T(8,128)S(1)}, u32[]{:S(2)}, u32[]{:S(2)}) %collective-permute-start.1) | collective-permute-done | bytes 65568 | tf_op jit(solution)/shard_map/ppermute | solution.py:141
  8.1 2.1 %collective-permute-start.2 = (f32[2,2,8,512]{3,2,1,0:T(8,128)S(1)}, f32[2,2,8,512]{3,2,1,0:T(8,128)S(1)}, u32[]{:S(2)}, u32[]{:S(2)}) collective-permute-start(f32[2,2,8,512]{3,2,1,0:T(8,128)S(1)} %collective-permute-done.1.refs_2_), channel_id=1, source_target_pairs={{0,4},{4,0},{8,12},{12,8},{1,5},{5,1},{9,13},{13,9},{2,6},{6,2},{1... | collective-permute-start | bytes 196616 | tf_op jit(solution)/shard_map/ppermute | solution.py:145
  10.2 0.1 collective-permute-done.refs_1_
  10.3 0.1 collective-permute-start.8
  10.4 1.6 %collective-permute-start.6 = (f32[6,2,4,512]{3,2,1,0:T(4,128)S(1)}, f32[6,2,4,512]{3,2,1,0:T(4,128)S(1)}, u32[]{:S(2)}, u32[]{:S(2)}) collective-permute-start(f32[6,2,4,512]{3,2,1,0:T(4,128)S(1)} %get-tuple-element.6), channel_id=1, source_target_pairs={{0,1},{1,0},{2,3},{3,2},{4,5},{5,4},{6,7},{7,6},{8,9},{9,8},{10,11... | collective-permute-start | bytes 294920 | tf_op jit(solution)/shard_map/ppermute | solution.py:135
  12.0 0.5 %collective-permute-done.4.refs_6_ = f32[2,2,8,512]{3,2,1,0:T(8,128)S(1)} collective-permute-done((f32[2,2,8,512]{3,2,1,0:T(8,128)S(1)}, f32[2,2,8,512]{3,2,1,0:T(8,128)S(1)}, u32[]{:S(2)}, u32[]{:S(2)}) %collective-permute-start.4) | collective-permute-done | bytes 65568 | tf_op jit(solution)/shard_map/ppermute | solution.py:143
  12.5 0.9 %collective-permute-start.5 = (f32[2,2,8,512]{3,2,1,0:T(8,128)S(1)}, f32[2,2,8,512]{3,2,1,0:T(8,128)S(1)}, u32[]{:S(2)}, u32[]{:S(2)}) collective-permute-start(f32[2,2,8,512]{3,2,1,0:T(8,128)S(1)} %collective-permute-done.4.refs_6_), channel_id=1, source_target_pairs={{0,4},{4,0},{8,12},{12,8},{1,5},{5,1},{9,13},{13,9},{2,6},{6,2},{1... | collective-permute-start | bytes 196616 | tf_op jit(solution)/shard_map/ppermute | solution.py:147
  13.4 0.1 collective-permute-done.2.refs_3_
  13.6 0.4 %collective-permute-start.9 = (f32[2,2,4,512]{3,2,1,0:T(4,128)S(1)}, f32[2,2,4,512]{3,2,1,0:T(4,128)S(1)}, u32[]{:S(2)}, u32[]{:S(2)}) collective-permute-start(f32[2,2,4,512]{3,2,1,0:T(4,128)S(1)} %get-tuple-element.9), channel_id=1, source_target_pairs={{1,2},{3,0},{2,1},{0,3},{5,6},{7,4},{6,5},{4,7},{9,10},{11,8},{10,... | collective-permute-start | bytes 98312 | tf_op jit(solution)/shard_map/ppermute | solution.py:136
  13.9 0.0 collective-permute-done.3.refs_5_
  13.9 0.0 copy-start
  13.9 1.3 %collective-permute-start.7 = (f32[2,2,4,512]{3,2,1,0:T(4,128)S(1)}, f32[2,2,4,512]{3,2,1,0:T(4,128)S(1)}, u32[]{:S(2)}, u32[]{:S(2)}) collective-permute-start(f32[2,2,4,512]{3,2,1,0:T(4,128)S(1)} %get-tuple-element.10), channel_id=1, source_target_pairs={{0,1},{1,0},{2,3},{3,2},{4,5},{5,4},{6,7},{7,6},{8,9},{9,8},{10,11... | collective-permute-start | bytes 98312 | tf_op jit(solution)/shard_map/ppermute | solution.py:135
  15.2 0.1 fusion.refs_12_
  15.3 1.5 %collective-permute-done.5.refs_7_ = f32[2,2,8,512]{3,2,1,0:T(8,128)S(1)} collective-permute-done((f32[2,2,8,512]{3,2,1,0:T(8,128)S(1)}, f32[2,2,8,512]{3,2,1,0:T(8,128)S(1)}, u32[]{:S(2)}, u32[]{:S(2)}) %collective-permute-start.5) | collective-permute-done | bytes 65568 | tf_op jit(solution)/shard_map/ppermute | solution.py:147
  16.8 0.5 %collective-permute-done.9.refs_11_ = f32[2,2,4,512]{3,2,1,0:T(4,128)S(1)} collective-permute-done((f32[2,2,4,512]{3,2,1,0:T(4,128)S(1)}, f32[2,2,4,512]{3,2,1,0:T(4,128)S(1)}, u32[]{:S(2)}, u32[]{:S(2)}) %collective-permute-start.9) | collective-permute-done | bytes 32800 | tf_op jit(solution)/shard_map/ppermute | solution.py:136
  17.3 0.0 collective-permute-done.7.refs_9_
  17.3 0.0 collective-permute-done.8.refs_10_
  17.3 0.0 collective-permute-done.6.refs_8_
  17.3 0.0 copy-done
  17.3 2.9 %coherence.1 = f32[2,8,2,16,512]{4,3,2,1,0:T(8,128)} custom-call(s32[8]{0:T(128)S(1)} %copy-done, f32[2,2,8,512]{3,2,1,0:T(8,128)S(1)} %pad_maximum_fusion.1.refs_0_, f32[2,2,8,512]{3,2,1,0:T(8,128)S(1)} %collective-permute-done.refs_1_, f32[2,2,8,512]{3,2,1,0:T(8,128)S(1)} %collective-permute-done.1.refs_2_, ...), custom_call_target="tpu_custom_call" | custom-call | tf_op jit(solution)/shard_map/coherence/pallas_call | solution.py:181
  (5 shorter events, 0.1 us)
Async XLA Ops:
  0.0 6.6 %copy-start.1 = (f32[2,2,16,512]{3,2,1,0:T(8,128)S(1)}, f32[2,2,16,512]{3,2,1,0:T(8,128)}, u32[]{:S(2)}) copy-start(f32[2,2,16,512]{3,2,1,0:T(8,128)} %param.2) | copy-start | bytes 393220
  1.0 7.2 %collective-permute-start.1 = (f32[2,2,8,512]{3,2,1,0:T(8,128)S(1)}, f32[2,2,8,512]{3,2,1,0:T(8,128)S(1)}, u32[]{:S(2)}, u32[]{:S(2)}) collective-permute-start(f32[2,2,8,512]{3,2,1,0:T(8,128)S(1)} %pad_maximum_fusion.1.refs_0_), channel_id=1, source_target_pairs={{0,8},{4,12},{8,0},{12,4},{1,9},{5,13},{9,1},{13,5},{2,10},{6,14},... | collective-permute-start | bytes 196616 | tf_op jit(solution)/shard_map/ppermute | solution.py:141
  5.1 5.2 %collective-permute-start = (f32[2,2,8,512]{3,2,1,0:T(8,128)S(1)}, f32[2,2,8,512]{3,2,1,0:T(8,128)S(1)}, u32[]{:S(2)}, u32[]{:S(2)}) collective-permute-start(f32[2,2,8,512]{3,2,1,0:T(8,128)S(1)} %pad_maximum_fusion.1.refs_0_), channel_id=1, source_target_pairs={{0,4},{4,0},{8,12},{12,8},{1,5},{5,1},{9,13},{13,9},{2,6},{6,2},{1... | collective-permute-start | bytes 196616 | tf_op jit(solution)/shard_map/ppermute | solution.py:142
  6.7 5.9 %collective-permute-start.4 = (f32[2,2,8,512]{3,2,1,0:T(8,128)S(1)}, f32[2,2,8,512]{3,2,1,0:T(8,128)S(1)}, u32[]{:S(2)}, u32[]{:S(2)}) collective-permute-start(f32[2,2,8,512]{3,2,1,0:T(8,128)S(1)} %slice.23.refs_4_), channel_id=1, source_target_pairs={{0,8},{4,12},{8,0},{12,4},{1,9},{5,13},{9,1},{13,5},{2,10},{6,14},... | collective-permute-start | bytes 196616 | tf_op jit(solution)/shard_map/ppermute | solution.py:143
  7.1 6.9 %collective-permute-start.3 = (f32[2,2,8,512]{3,2,1,0:T(8,128)S(1)}, f32[2,2,8,512]{3,2,1,0:T(8,128)S(1)}, u32[]{:S(2)}, u32[]{:S(2)}) collective-permute-start(f32[2,2,8,512]{3,2,1,0:T(8,128)S(1)} %slice.23.refs_4_), channel_id=1, source_target_pairs={{0,4},{4,0},{8,12},{12,8},{1,5},{5,1},{9,13},{13,9},{2,6},{6,2},{1... | collective-permute-start | bytes 196616 | tf_op jit(solution)/shard_map/ppermute | solution.py:144
  8.1 5.4 %collective-permute-start.2 = (f32[2,2,8,512]{3,2,1,0:T(8,128)S(1)}, f32[2,2,8,512]{3,2,1,0:T(8,128)S(1)}, u32[]{:S(2)}, u32[]{:S(2)}) collective-permute-start(f32[2,2,8,512]{3,2,1,0:T(8,128)S(1)} %collective-permute-done.1.refs_2_), channel_id=1, source_target_pairs={{0,4},{4,0},{8,12},{12,8},{1,5},{5,1},{9,13},{13,9},{2,6},{6,2},{1... | collective-permute-start | bytes 196616 | tf_op jit(solution)/shard_map/ppermute | solution.py:145
  10.3 6.9 %collective-permute-start.8 = (f32[6,2,4,512]{3,2,1,0:T(4,128)S(1)}, f32[6,2,4,512]{3,2,1,0:T(4,128)S(1)}, u32[]{:S(2)}, u32[]{:S(2)}) collective-permute-start(f32[6,2,4,512]{3,2,1,0:T(4,128)S(1)} %get-tuple-element.5), channel_id=1, source_target_pairs={{1,2},{3,0},{2,1},{0,3},{5,6},{7,4},{6,5},{4,7},{9,10},{11,8},{10,... | collective-permute-start | bytes 294920 | tf_op jit(solution)/shard_map/ppermute | solution.py:136
  10.4 6.9 %collective-permute-start.6 = (f32[6,2,4,512]{3,2,1,0:T(4,128)S(1)}, f32[6,2,4,512]{3,2,1,0:T(4,128)S(1)}, u32[]{:S(2)}, u32[]{:S(2)}) collective-permute-start(f32[6,2,4,512]{3,2,1,0:T(4,128)S(1)} %get-tuple-element.6), channel_id=1, source_target_pairs={{0,1},{1,0},{2,3},{3,2},{4,5},{5,4},{6,7},{7,6},{8,9},{9,8},{10,11... | collective-permute-start | bytes 294920 | tf_op jit(solution)/shard_map/ppermute | solution.py:135
  12.5 4.3 %collective-permute-start.5 = (f32[2,2,8,512]{3,2,1,0:T(8,128)S(1)}, f32[2,2,8,512]{3,2,1,0:T(8,128)S(1)}, u32[]{:S(2)}, u32[]{:S(2)}) collective-permute-start(f32[2,2,8,512]{3,2,1,0:T(8,128)S(1)} %collective-permute-done.4.refs_6_), channel_id=1, source_target_pairs={{0,4},{4,0},{8,12},{12,8},{1,5},{5,1},{9,13},{13,9},{2,6},{6,2},{1... | collective-permute-start | bytes 196616 | tf_op jit(solution)/shard_map/ppermute | solution.py:147
  13.6 3.7 %collective-permute-start.9 = (f32[2,2,4,512]{3,2,1,0:T(4,128)S(1)}, f32[2,2,4,512]{3,2,1,0:T(4,128)S(1)}, u32[]{:S(2)}, u32[]{:S(2)}) collective-permute-start(f32[2,2,4,512]{3,2,1,0:T(4,128)S(1)} %get-tuple-element.9), channel_id=1, source_target_pairs={{1,2},{3,0},{2,1},{0,3},{5,6},{7,4},{6,5},{4,7},{9,10},{11,8},{10,... | collective-permute-start | bytes 98312 | tf_op jit(solution)/shard_map/ppermute | solution.py:136
  13.9 3.4 %copy-start = (s32[8]{0:T(128)S(1)}, s32[8]{0:T(128)}, u32[]{:S(2)}) copy-start(s32[8]{0:T(128)} %plan_ref.1) | copy-start | bytes 100
  13.9 3.3 %collective-permute-start.7 = (f32[2,2,4,512]{3,2,1,0:T(4,128)S(1)}, f32[2,2,4,512]{3,2,1,0:T(4,128)S(1)}, u32[]{:S(2)}, u32[]{:S(2)}) collective-permute-start(f32[2,2,4,512]{3,2,1,0:T(4,128)S(1)} %get-tuple-element.10), channel_id=1, source_target_pairs={{0,1},{1,0},{2,3},{3,2},{4,5},{5,4},{6,7},{7,6},{8,9},{9,8},{10,11... | collective-permute-start | bytes 98312 | tf_op jit(solution)/shard_map/ppermute | solution.py:135

commit v3 on v0

v3 whole, which is shorter than its diff:
```python
import functools

import jax
import jax.numpy as jnp
from jax import lax
from jax.experimental import pallas as pl
from jax.experimental.pallas import tpu as pltpu
from jax.sharding import PartitionSpec as P

HALF_ROWS = 4
HALF_COLS = 16
epsilon = 1e-06


def split(x):
    high = x.astype(jnp.bfloat16)
    low = (x - high.astype(jnp.float32)).astype(jnp.bfloat16)
    return high, low


def row_window(f, rows):
    length = f.shape[0]
    total, width = f, 1
    while width < 2 * HALF_ROWS:
        total = total + pltpu.roll(total, length - width, 0)
        width *= 2
    return total[:rows] + f[2 * HALF_ROWS:]


def kernel(counts, nd, own, stage, n_rows, *refs):
    def take(n):
        nonlocal refs
        head, refs = refs[:n], refs[n:]
        return head

    (plan_ref,) = take(0 if stage == "early" else 1)[:1] or (None,)
    own_ref, own_power, done = take(3) if stage == "last" else (None,) * 3
    edges, inners, rim_x, rim_c = (take(len(counts[n])) for n in (0, 0, 2, 1))
    (band_ref,) = take(1)
    if stage == "early":
        own_ref, own_power, buf, ext, res = refs
    elif stage == "last":
        out_ref, ext, res, buf, sems = refs
    else:
        out_ref, ext, res, buf, own_ref, own_power, sems = refs
    half = HALF_ROWS
    rows = inners[0].shape[2] + 2 * half
    first = nd if stage == "all" else 0
    slots = sum(counts[0]) - first
    row = lax.axis_index("row")
    odd = row % 2 == 1
    copies = []

    if stage == "last":
        listed = plan_ref[...]
        slot_of = ((listed // nd) ^ lax.axis_index("date")) * nd + listed % nd
        digits = (listed.shape[1] - 1).bit_length()
        each = 31 // digits
        lane = lax.broadcasted_iota(jnp.int32, listed.shape, 1)
        words = [
            jnp.sum(jnp.where(slot_of // each == w, lane << (slot_of % each * digits), 0))
            for w in range(-(-listed.shape[1] // each))
        ]

    def place(slot, date):
        if stage == "last":
            return (words[slot // each] >> (slot % each * digits)) & ((1 << digits) - 1)
        listed = plan_ref[...]
        lane = lax.broadcasted_iota(jnp.int32, listed.shape, 1)
        return jnp.sum(jnp.where(listed == date, lane, 0))

    def send(ref, slot):
        if stage == "all":
            date = pl.program_id(0) * slots + slot
        else:
            date = (lax.axis_index("date") ^ (slot // nd)) * nd + slot % nd
        k = place(slot, date)
        for d in range(nd):
            copy = pltpu.make_async_copy(ref[d], out_ref.at[d, k], sems.at[d, slot])
            copy.start()
            copies.append(copy)

    at = 0
    for ref, inner, count in zip(edges, inners, counts[0]):
        for d in range(count):
            to = own_ref.at[at] if stage != "last" and at < nd else ext.at[at]
            to[:, half:2 * half] = ref[d, :, half:]
            to[:, 2 * half:rows] = inner[d]
            to[:, rows:rows + half] = ref[d, :, :half]
            at += 1
    near = [r.at[d] for r, count in zip(rim_c, counts[1]) for d in range(count)]
    far = [r.at[d] for r, count in zip(rim_x, counts[2]) for d in range(count)]
    for at, (c, x) in enumerate(zip(near, far)):
        to = own_ref.at[at] if stage != "last" and at < nd else ext.at[at]
        top = jnp.where(odd, c[...], x[...])
        bottom = jnp.where(odd, x[...], c[...])
        to[:, :half] = jnp.where(row == 0, 0.0, top)
        to[:, rows + half:] = jnp.where(row == n_rows - 1, 0.0, bottom)

    band = band_ref[...]

    def columns(fields):
        high, low = zip(*(split(f) for f in fields))
        both = jnp.concatenate(high + low, axis=0)
        out = jnp.dot(both, band, preferred_element_type=jnp.float32)
        middle = out.shape[0] // 2
        return out[:middle] + out[middle:]

    def power_of(re, im):
        return row_window(re * re + im * im, rows)

    def cross_of(mr, mi, re, im):
        return [row_window(mr * re + mi * im, rows), row_window(mi * re - mr * im, rows)]

    def scale(a, b):
        return lax.rsqrt(a * b + epsilon)

    if stage != "last":
        fields = [power_of(own_ref[d, 0], own_ref[d, 1]) for d in range(nd)]
        pairs = [(d, s) for s in range(nd) for d in range(s)] if stage == "early" else []
        for d, s in pairs:
            fields += cross_of(own_ref[d, 0], own_ref[d, 1], own_ref[s, 0], own_ref[s, 1])
        sums = columns(fields)
        for d in range(nd):
            own_power[d] = sums[d * rows:(d + 1) * rows]
        if stage == "early":
            for d in range(nd):
                power = own_power[d]
                buf[d, d, 0] = power * scale(power, power)
                buf[d, d, 1] = jnp.zeros_like(power)
            for n, (d, s) in enumerate(pairs):
                at = (nd + 2 * n) * rows
                factor = scale(own_power[d], own_power[s])
                real, imag = sums[at:at + rows] * factor, sums[at + rows:at + 2 * rows] * factor
                buf[d, s, 0], buf[d, s, 1] = real, imag
                buf[s, d, 0], buf[s, d, 1] = real, -imag

    for s in range(nd if stage == "early" else 0, slots):
        re, im = ext[first + s, 0], ext[first + s, 1]
        fields = [power_of(re, im)]
        for d in range(nd):
            fields += cross_of(own_ref[d, 0], own_ref[d, 1], re, im)
        res[s] = columns(fields)
        power = res[s, :rows]
        for d in range(nd):
            factor = scale(own_power[d], power)
            at = (1 + 2 * d) * rows
            buf[d, s, 0] = res[s, at:at + rows] * factor
            buf[d, s, 1] = res[s, at + rows:at + 2 * rows] * factor
        if stage == "last" and s == 0:
            for t in range(own):
                send([done.at[d, t] for d in range(nd)], t)
        if stage != "early":
            send([buf.at[d, s] for d in range(nd)], own + s)
    for copy in copies:
        copy.wait()


def pairs_of(size, flip):
    return [(i, i ^ flip) for i in range(size)]


def body(stack_data, plan):
    nd, _, rows, cols = stack_data.shape
    size, n_rows = lax.axis_size("date"), lax.axis_size("row")
    half = HALF_ROWS
    odd = lax.axis_index("row") % 2 == 1

    near = [(i, i ^ 1) for i in range(n_rows) if (i ^ 1) < n_rows]
    far = [(i, (i + 1) % n_rows) for i in range(1, n_rows, 2)] if n_rows % 2 == 0 else [
        (i, i + 1) for i in range(1, n_rows - 1, 2)]
    far = far + [(j, i) for i, j in far if i != j]

    def cut(block):
        first, last = block[:, :, :half], block[:, :, rows - half:]
        return jnp.concatenate([last, first], axis=2), block[:, :, half:rows - half]

    def rim_near(edge):
        last, first = edge[:, :, :half], edge[:, :, half:]
        return lax.ppermute(jnp.where(odd, first, last), "row", near)

    def rim_far(edge):
        last, first = edge[:, :, :half], edge[:, :, half:]
        return lax.ppermute(jnp.where(odd, last, first), "row", far)

    def z(array, flip):
        return lax.ppermute(array, "date", pairs_of(size, flip))

    def after(array, *others):
        return lax.optimization_barrier((array,) + others)[0]

    def join(*blocks):
        return jnp.concatenate(blocks, axis=0)

    out_col = lax.broadcasted_iota(jnp.int32, (cols, cols), 0)
    in_col = lax.broadcasted_iota(jnp.int32, (cols, cols), 1)
    band = (jnp.abs(out_col - in_col) <= HALF_COLS).astype(jnp.bfloat16)
    out_shape = jax.ShapeDtypeStruct((nd, size * nd, 2, rows, cols), jnp.float32)
    own_shape = (nd, 2, rows + 2 * half, cols)
    power_shape = (nd, rows, cols)
    vmem = pl.BlockSpec(memory_space=pltpu.VMEM)
    listed = jnp.maximum(plan, 0).reshape(1, -1)
    hbm = pl.BlockSpec(memory_space=pl.ANY)

    def scratch(total, slots):
        return [
            pltpu.VMEM((total, 2, rows + 2 * half, cols), jnp.float32),
            pltpu.VMEM((slots, (1 + 2 * nd) * rows, cols), jnp.float32),
            pltpu.VMEM((nd, slots, 2, rows, cols), jnp.float32),
        ]

    def work(slots):
        pairs = slots * nd * rows * cols
        return pl.CostEstimate(flops=16 * pairs * cols, bytes_accessed=16 * pairs, transcendentals=pairs)

    params = pltpu.CompilerParams(vmem_limit_bytes=32 * 2**20)
    edge, inner = cut(stack_data)
    if size == 4:
        edge_2 = z(edge, 2)
        edge_1 = z(edge, 1)
        inner_2 = z(inner, 2)
        inner_1 = z(inner, 1)
        edge_3 = z(edge_2, 1)
        inner_3 = z(inner_2, 1)
        early = join(edge, edge_1, edge_2)
        near_a, far_a = rim_near(early), rim_far(early)
        near_b, far_b = rim_near(edge_3), rim_far(edge_3)
        slots = 3 * nd
        operands = [edge, edge_1, edge_2, inner, inner_1, inner_2, far_a, near_a, band]
        own, power, done = pl.pallas_call(
            functools.partial(kernel, ([nd] * 3, [slots], [slots]), nd, 0, "early", n_rows),
            out_shape=[
                jax.ShapeDtypeStruct(own_shape, jnp.float32),
                jax.ShapeDtypeStruct(power_shape, jnp.float32),
                jax.ShapeDtypeStruct((nd, slots, 2, rows, cols), jnp.float32),
            ],
            in_specs=[vmem] * len(operands),
            out_specs=[vmem] * 3,
            scratch_shapes=scratch(slots, slots)[:2],
            compiler_params=params,
            cost_estimate=work(slots),
            name="early_dates",
        )(*operands)
        operands = [listed, own, power, done, edge_3, inner_3, far_b, near_b, band]
        return pl.pallas_call(
            functools.partial(kernel, ([nd], [nd], [nd]), nd, slots, "last", n_rows),
            out_shape=out_shape,
            in_specs=[vmem] * len(operands),
            out_specs=hbm,
            scratch_shapes=scratch(nd, nd) + [pltpu.SemaphoreType.DMA((nd, size * nd))],
            compiler_params=params,
            cost_estimate=work(nd),
            name="last_dates",
        )(*operands)

    gathered = lax.all_gather(stack_data, "date", axis=0, tiled=True)
    all_edge, all_inner = cut(gathered)
    operands = [edge, all_edge, inner, all_inner, rim_far(edge), rim_far(all_edge), rim_near(edge), rim_near(all_edge)]
    slots = next(n for n in (8, 4, 2, 1) if (size * nd) % n == 0)

    def spec(array, chunk):
        if chunk:
            return pl.BlockSpec((slots,) + array.shape[1:], lambda g: (g, 0, 0, 0))
        return pl.BlockSpec(array.shape, lambda g: (0,) * array.ndim)

    return pl.pallas_call(
        functools.partial(kernel, ([nd, slots],) * 3, nd, 0, "all", n_rows),
        grid=(size * nd // slots,),
        out_shape=out_shape,
        in_specs=[vmem] + [spec(a, n % 2) for n, a in enumerate(operands)] + [spec(band, 0)],
        out_specs=hbm,
        scratch_shapes=scratch(nd + slots, slots)
        + [
            pltpu.VMEM(own_shape, jnp.float32),
            pltpu.VMEM(power_shape, jnp.float32),
            pltpu.SemaphoreType.DMA((nd, slots)),
        ],
        compiler_params=params,
        name="all_dates",
    )(listed, *operands, band)


def solution(mesh):
    placed = (P(("grp", "date"), None, "row", None), P())
    return jax.shard_map(
        body,
        mesh=mesh,
        in_specs=placed,
        out_specs=P(("grp", "date"), None, None, "row", None),
        check_vma=False,
    )
```

time: 34.4 us -> 18.8 us (0.55)
  the two profiles are of different devices: /device:TPU:1 before, /device:TPU:0 now
where the time goes in v3:
time: 18.8 us; the launch traced here: 18.6 us
  starting transfers between devices  12.6 us (67%)
  Pallas kernels  2.44 us (13%)
  waiting for transfers between devices  1.73 us (9%)
  local copies, waits for them, and re-layouts  1.6 us (9%)
    ppermute x6, starting transfers between devices, z(): return lax.ppermute(array, 'date', pairs_of(size, flip))  9.22 us
    ppermute x2, starting transfers between devices, rim_far(): return lax.ppermute(jnp.where(odd, last, first), 'row', far)  3.21 us
    pallas_call x1, Pallas kernels, body(): pl.pallas_call(functools.partial(kernel, ([nd], [nd], [nd]), nd, slots, '...  1.54 us
    ppermute x6, waiting for transfers between devices, z(): return lax.ppermute(array, 'date', pairs_of(size, flip))  1.46 us
    slice x1, local copies, waits for them, and re-layouts, cut(): first, last = (block[:, :, :half], block[:, :, rows - half:])  0.93 us
    pallas_call x1, Pallas kernels, body(): pl.pallas_call(functools.partial(kernel, ([nd] * 3, [slots], [slots]), nd...  0.91 us
    unnamed x4, local copies, waits for them, and re-layouts  0.66 us
  transfers between devices with their start and end apart: 10, of which 6 were waited for; matrix products, arithmetic and copies ran while one was open for 1% of the time, Pallas kernels for 5%

profile of v3, /device:TPU:0, one launch (start us, length us, event | category | flops | bytes accessed | tf_op | source)
XLA Modules:
  0.0 18.6 jit_solution(12089636603097253922)
XLA Ops:
  0.0 0.0 copy-start
  0.0 0.9 %fusion.1 = (f32[2,2,4,512]{3,2,1,0:T(4,128)S(1)}, f32[2,2,4,512]{3,2,1,0:T(4,128)S(1)}) fusion(f32[2,2,16,512]{3,2,1,0:T(8,128)} %param.2), kind=kLoop, calls=%fused_computation.9 | loop fusion | bytes 131072 | tf_op jit(solution)/shard_map/slice | solution.py:175
  1.0 4.1 %collective-permute-start.1 = (f32[2,2,8,512]{3,2,1,0:T(8,128)S(1)}, f32[2,2,8,512]{3,2,1,0:T(8,128)S(1)}, u32[]{:S(2)}, u32[]{:S(2)}) collective-permute-start(f32[2,2,8,512]{3,2,1,0:T(8,128)S(1)} %pad_maximum_fusion.1.refs_0_), channel_id=1, source_target_pairs={{0,8},{4,12},{8,0},{12,4},{1,9},{5,13},{9,1},{13,5},{2,10},{6,14},... | collective-permute-start | bytes 196616 | tf_op jit(solution)/shard_map/ppermute | solution.py:187
  5.1 1.6 %collective-permute-start = (f32[2,2,8,512]{3,2,1,0:T(8,128)S(1)}, f32[2,2,8,512]{3,2,1,0:T(8,128)S(1)}, u32[]{:S(2)}, u32[]{:S(2)}) collective-permute-start(f32[2,2,8,512]{3,2,1,0:T(8,128)S(1)} %pad_maximum_fusion.1.refs_0_), channel_id=1, source_target_pairs={{0,4},{4,0},{8,12},{12,8},{1,5},{5,1},{9,13},{13,9},{2,6},{6,2},{1... | collective-permute-start | bytes 196616 | tf_op jit(solution)/shard_map/ppermute | solution.py:187
  6.6 0.0 copy-done
  6.7 0.4 %collective-permute-start.3 = (f32[2,2,8,512]{3,2,1,0:T(8,128)S(1)}, f32[2,2,8,512]{3,2,1,0:T(8,128)S(1)}, u32[]{:S(2)}, u32[]{:S(2)}) collective-permute-start(f32[2,2,8,512]{3,2,1,0:T(8,128)S(1)} %slice.27.refs_3_), channel_id=1, source_target_pairs={{0,8},{4,12},{8,0},{12,4},{1,9},{5,13},{9,1},{13,5},{2,10},{6,14},... | collective-permute-start | bytes 196616 | tf_op jit(solution)/shard_map/ppermute | solution.py:187
  7.1 0.2 %collective-permute-start.2 = (f32[2,2,8,512]{3,2,1,0:T(8,128)S(1)}, f32[2,2,8,512]{3,2,1,0:T(8,128)S(1)}, u32[]{:S(2)}, u32[]{:S(2)}) collective-permute-start(f32[2,2,8,512]{3,2,1,0:T(8,128)S(1)} %slice.27.refs_3_), channel_id=1, source_target_pairs={{0,4},{4,0},{8,12},{12,8},{1,5},{5,1},{9,13},{13,9},{2,6},{6,2},{1... | collective-permute-start | bytes 196616 | tf_op jit(solution)/shard_map/ppermute | solution.py:187
  7.2 0.0 copy-start.1
  7.3 0.7 %copy-done.1 = s32[8]{0:T(128)S(1)} copy-done((s32[8]{0:T(128)S(1)}, s32[8]{0:T(128)}, u32[]{:S(2)}) %copy-start.1) | copy-done | bytes 56
  7.9 0.1 fusion.refs_8_
  8.0 0.1 collective-permute-done.1.refs_2_
  8.1 2.1 %collective-permute-start.6 = (f32[2,2,8,512]{3,2,1,0:T(8,128)S(1)}, f32[2,2,8,512]{3,2,1,0:T(8,128)S(1)}, u32[]{:S(2)}, u32[]{:S(2)}) collective-permute-start(f32[2,2,8,512]{3,2,1,0:T(8,128)S(1)} %collective-permute-done.1.refs_2_), channel_id=1, source_target_pairs={{0,4},{4,0},{8,12},{12,8},{1,5},{5,1},{9,13},{13,9},{2,6},{6,2},{1... | collective-permute-start | bytes 196616 | tf_op jit(solution)/shard_map/ppermute | solution.py:187
  10.2 0.1 collective-permute-done.refs_1_
  10.3 0.1 collective-permute-start.5
  10.4 1.6 %collective-permute-start.4 = (f32[6,2,4,512]{3,2,1,0:T(4,128)S(1)}, f32[6,2,4,512]{3,2,1,0:T(4,128)S(1)}, u32[]{:S(2)}, u32[]{:S(2)}) collective-permute-start(f32[6,2,4,512]{3,2,1,0:T(4,128)S(1)} %get-tuple-element.12), channel_id=1, source_target_pairs={{1,2},{3,0},{2,1},{0,3},{5,6},{7,4},{6,5},{4,7},{9,10},{11,8},{10,... | collective-permute-start | bytes 294920 | tf_op jit(solution)/shard_map/ppermute | solution.py:184
  12.0 0.5 %collective-permute-done.3.refs_5_ = f32[2,2,8,512]{3,2,1,0:T(8,128)S(1)} collective-permute-done((f32[2,2,8,512]{3,2,1,0:T(8,128)S(1)}, f32[2,2,8,512]{3,2,1,0:T(8,128)S(1)}, u32[]{:S(2)}, u32[]{:S(2)}) %collective-permute-start.3) | collective-permute-done | bytes 65568 | tf_op jit(solution)/shard_map/ppermute | solution.py:187
  12.5 0.9 %collective-permute-start.7 = (f32[2,2,8,512]{3,2,1,0:T(8,128)S(1)}, f32[2,2,8,512]{3,2,1,0:T(8,128)S(1)}, u32[]{:S(2)}, u32[]{:S(2)}) collective-permute-start(f32[2,2,8,512]{3,2,1,0:T(8,128)S(1)} %collective-permute-done.3.refs_5_), channel_id=1, source_target_pairs={{0,4},{4,0},{8,12},{12,8},{1,5},{5,1},{9,13},{13,9},{2,6},{6,2},{1... | collective-permute-start | bytes 196616 | tf_op jit(solution)/shard_map/ppermute | solution.py:187
  13.4 0.1 collective-permute-done.6.refs_4_
  13.6 0.1 collective-permute-start.9
  13.6 0.0 collective-permute-done.2.refs_4_
  13.6 1.6 %collective-permute-start.8 = (f32[2,2,4,512]{3,2,1,0:T(4,128)S(1)}, f32[2,2,4,512]{3,2,1,0:T(4,128)S(1)}, u32[]{:S(2)}, u32[]{:S(2)}) collective-permute-start(f32[2,2,4,512]{3,2,1,0:T(4,128)S(1)} %get-tuple-element.16), channel_id=1, source_target_pairs={{1,2},{3,0},{2,1},{0,3},{5,6},{7,4},{6,5},{4,7},{9,10},{11,8},{10,... | collective-permute-start | bytes 98312 | tf_op jit(solution)/shard_map/ppermute | solution.py:184
  15.2 0.0 collective-permute-done.5.refs_7_
  15.2 0.0 collective-permute-done.4.refs_6_
  15.3 0.9 %early_dates.1 = (f32[2,2,24,512]{3,2,1,0:T(8,128)S(1)}, f32[2,16,512]{2,1,0:T(8,128)S(1)}, f32[2,6,2,16,512]{4,3,2,1,0:T(8,128)S(1)}) custom-call(f32[2,2,8,512]{3,2,1,0:T(8,128)S(1)} %pad_maximum_fusion.1.refs_0_, f32[2,2,8,512]{3,2,1,0:T(8,128)S(1)} %collective-permute-done.refs_1_, f32[2,2,8,512]{3,2,1,0:T(8,128)S(1)} %collective-permute-done.1.refs_2_, ...), custom_call_target="tpu_custom_call" | custom-call | flops 805306368 | bytes 1572864 | tf_op jit(solution)/shard_map/early_dates/pallas_call | solution.py:230
  16.2 0.6 %collective-permute-done.7.refs_5_ = f32[2,2,8,512]{3,2,1,0:T(8,128)S(1)} collective-permute-done((f32[2,2,8,512]{3,2,1,0:T(8,128)S(1)}, f32[2,2,8,512]{3,2,1,0:T(8,128)S(1)}, u32[]{:S(2)}, u32[]{:S(2)}) %collective-permute-start.7) | collective-permute-done | bytes 65568 | tf_op jit(solution)/shard_map/ppermute | solution.py:187
  16.8 0.0 collective-permute-done.9.refs_7_
  16.8 0.3 %collective-permute-done.8.refs_6_ = f32[2,2,4,512]{3,2,1,0:T(4,128)S(1)} collective-permute-done((f32[2,2,4,512]{3,2,1,0:T(4,128)S(1)}, f32[2,2,4,512]{3,2,1,0:T(4,128)S(1)}, u32[]{:S(2)}, u32[]{:S(2)}) %collective-permute-start.8) | collective-permute-done | bytes 32800 | tf_op jit(solution)/shard_map/ppermute | solution.py:184
  17.1 1.5 %last_dates.1 = f32[2,8,2,16,512]{4,3,2,1,0:T(8,128)} custom-call(s32[1,8]{1,0:T(1,128)S(1)} %maximum_bitcast_fusion.refs_0_, f32[2,2,24,512]{3,2,1,0:T(8,128)S(1)} %get-tuple-element.8.refs_1_, f32[2,16,512]{2,1,0:T(8,128)S(1)} %get-tuple-element.9.refs_2_, f32[2,6,2,16,512]{4,3,2,1,0:T(8,128)S(1)} %get-tuple-element.10.refs_3_, ...), custom_call_target="tpu_custom_call" | custom-call | flops 268435456 | bytes 524288 | tf_op jit(solution)/shard_map/last_dates/pallas_call | solution.py:245
  (6 shorter events, 0.1 us)
Async XLA Ops:
  0.0 6.6 %copy-start = (f32[2,2,16,512]{3,2,1,0:T(8,128)S(1)}, f32[2,2,16,512]{3,2,1,0:T(8,128)}, u32[]{:S(2)}) copy-start(f32[2,2,16,512]{3,2,1,0:T(8,128)} %param.2) | copy-start | bytes 393220
  1.0 7.2 %collective-permute-start.1 = (f32[2,2,8,512]{3,2,1,0:T(8,128)S(1)}, f32[2,2,8,512]{3,2,1,0:T(8,128)S(1)}, u32[]{:S(2)}, u32[]{:S(2)}) collective-permute-start(f32[2,2,8,512]{3,2,1,0:T(8,128)S(1)} %pad_maximum_fusion.1.refs_0_), channel_id=1, source_target_pairs={{0,8},{4,12},{8,0},{12,4},{1,9},{5,13},{9,1},{13,5},{2,10},{6,14},... | collective-permute-start | bytes 196616 | tf_op jit(solution)/shard_map/ppermute | solution.py:187
  5.1 5.2 %collective-permute-start = (f32[2,2,8,512]{3,2,1,0:T(8,128)S(1)}, f32[2,2,8,512]{3,2,1,0:T(8,128)S(1)}, u32[]{:S(2)}, u32[]{:S(2)}) collective-permute-start(f32[2,2,8,512]{3,2,1,0:T(8,128)S(1)} %pad_maximum_fusion.1.refs_0_), channel_id=1, source_target_pairs={{0,4},{4,0},{8,12},{12,8},{1,5},{5,1},{9,13},{13,9},{2,6},{6,2},{1... | collective-permute-start | bytes 196616 | tf_op jit(solution)/shard_map/ppermute | solution.py:187
  6.7 5.9 %collective-permute-start.3 = (f32[2,2,8,512]{3,2,1,0:T(8,128)S(1)}, f32[2,2,8,512]{3,2,1,0:T(8,128)S(1)}, u32[]{:S(2)}, u32[]{:S(2)}) collective-permute-start(f32[2,2,8,512]{3,2,1,0:T(8,128)S(1)} %slice.27.refs_3_), channel_id=1, source_target_pairs={{0,8},{4,12},{8,0},{12,4},{1,9},{5,13},{9,1},{13,5},{2,10},{6,14},... | collective-permute-start | bytes 196616 | tf_op jit(solution)/shard_map/ppermute | solution.py:187
  7.1 6.6 %collective-permute-start.2 = (f32[2,2,8,512]{3,2,1,0:T(8,128)S(1)}, f32[2,2,8,512]{3,2,1,0:T(8,128)S(1)}, u32[]{:S(2)}, u32[]{:S(2)}) collective-permute-start(f32[2,2,8,512]{3,2,1,0:T(8,128)S(1)} %slice.27.refs_3_), channel_id=1, source_target_pairs={{0,4},{4,0},{8,12},{12,8},{1,5},{5,1},{9,13},{13,9},{2,6},{6,2},{1... | collective-permute-start | bytes 196616 | tf_op jit(solution)/shard_map/ppermute | solution.py:187
  7.2 0.7 %copy-start.1 = (s32[8]{0:T(128)S(1)}, s32[8]{0:T(128)}, u32[]{:S(2)}) copy-start(s32[8]{0:T(128)} %param.3) | copy-start | bytes 100
  8.1 5.4 %collective-permute-start.6 = (f32[2,2,8,512]{3,2,1,0:T(8,128)S(1)}, f32[2,2,8,512]{3,2,1,0:T(8,128)S(1)}, u32[]{:S(2)}, u32[]{:S(2)}) collective-permute-start(f32[2,2,8,512]{3,2,1,0:T(8,128)S(1)} %collective-permute-done.1.refs_2_), channel_id=1, source_target_pairs={{0,4},{4,0},{8,12},{12,8},{1,5},{5,1},{9,13},{13,9},{2,6},{6,2},{1... | collective-permute-start | bytes 196616 | tf_op jit(solution)/shard_map/ppermute | solution.py:187
  10.3 4.9 %collective-permute-start.5 = (f32[6,2,4,512]{3,2,1,0:T(4,128)S(1)}, f32[6,2,4,512]{3,2,1,0:T(4,128)S(1)}, u32[]{:S(2)}, u32[]{:S(2)}) collective-permute-start(f32[6,2,4,512]{3,2,1,0:T(4,128)S(1)} %get-tuple-element.11), channel_id=1, source_target_pairs={{0,1},{1,0},{2,3},{3,2},{4,5},{5,4},{6,7},{7,6},{8,9},{9,8},{10,11... | collective-permute-start | bytes 294920 | tf_op jit(solution)/shard_map/ppermute | solution.py:180
  10.4 4.9 %collective-permute-start.4 = (f32[6,2,4,512]{3,2,1,0:T(4,128)S(1)}, f32[6,2,4,512]{3,2,1,0:T(4,128)S(1)}, u32[]{:S(2)}, u32[]{:S(2)}) collective-permute-start(f32[6,2,4,512]{3,2,1,0:T(4,128)S(1)} %get-tuple-element.12), channel_id=1, source_target_pairs={{1,2},{3,0},{2,1},{0,3},{5,6},{7,4},{6,5},{4,7},{9,10},{11,8},{10,... | collective-permute-start | bytes 294920 | tf_op jit(solution)/shard_map/ppermute | solution.py:184
  12.5 4.3 %collective-permute-start.7 = (f32[2,2,8,512]{3,2,1,0:T(8,128)S(1)}, f32[2,2,8,512]{3,2,1,0:T(8,128)S(1)}, u32[]{:S(2)}, u32[]{:S(2)}) collective-permute-start(f32[2,2,8,512]{3,2,1,0:T(8,128)S(1)} %collective-permute-done.3.refs_5_), channel_id=1, source_target_pairs={{0,4},{4,0},{8,12},{12,8},{1,5},{5,1},{9,13},{13,9},{2,6},{6,2},{1... | collective-permute-start | bytes 196616 | tf_op jit(solution)/shard_map/ppermute | solution.py:187
  13.6 3.2 %collective-permute-start.9 = (f32[2,2,4,512]{3,2,1,0:T(4,128)S(1)}, f32[2,2,4,512]{3,2,1,0:T(4,128)S(1)}, u32[]{:S(2)}, u32[]{:S(2)}) collective-permute-start(f32[2,2,4,512]{3,2,1,0:T(4,128)S(1)} %get-tuple-element.15), channel_id=1, source_target_pairs={{0,1},{1,0},{2,3},{3,2},{4,5},{5,4},{6,7},{7,6},{8,9},{9,8},{10,11... | collective-permute-start | bytes 98312 | tf_op jit(solution)/shard_map/ppermute | solution.py:180
  13.6 3.4 %collective-permute-start.8 = (f32[2,2,4,512]{3,2,1,0:T(4,128)S(1)}, f32[2,2,4,512]{3,2,1,0:T(4,128)S(1)}, u32[]{:S(2)}, u32[]{:S(2)}) collective-permute-start(f32[2,2,4,512]{3,2,1,0:T(4,128)S(1)} %get-tuple-element.16), channel_id=1, source_target_pairs={{1,2},{3,0},{2,1},{0,3},{5,6},{7,4},{6,5},{4,7},{9,10},{11,8},{10,... | collective-permute-start | bytes 98312 | tf_op jit(solution)/shard_map/ppermute | solution.py:184

commit v4 on v3

--- a/solution.py
+++ b/solution.py
@@ -27,18 +27,19 @@
     return total[:rows] + f[2 * HALF_ROWS:]
 
 
-def kernel(counts, nd, own, stage, n_rows, *refs):
+def kernel(counts, nd, own, stage, n_rows, digits, *refs):
     def take(n):
         nonlocal refs
         head, refs = refs[:n], refs[n:]
         return head
 
-    (plan_ref,) = take(0 if stage == "early" else 1)[:1] or (None,)
+    each = 31 // digits
+    (plan_ref,) = take(1)
     own_ref, own_power, done = take(3) if stage == "last" else (None,) * 3
-    edges, inners, rim_x, rim_c = (take(len(counts[n])) for n in (0, 0, 2, 1))
+    edges, inners, rim_c, rim_x = (take(len(counts[n])) for n in (0, 0, 1, 2))
     (band_ref,) = take(1)
     if stage == "early":
-        own_ref, own_power, buf, ext, res = refs
+        own_ref, own_power, buf, words_ref, ext, res = refs
     elif stage == "last":
         out_ref, ext, res, buf, sems = refs
     else:
@@ -51,16 +52,15 @@
     odd = row % 2 == 1
     copies = []
 
-    if stage == "last":
+    if stage == "early":
         listed = plan_ref[...]
         slot_of = ((listed // nd) ^ lax.axis_index("date")) * nd + listed % nd
-        digits = (listed.shape[1] - 1).bit_length()
-        each = 31 // digits
         lane = lax.broadcasted_iota(jnp.int32, listed.shape, 1)
-        words = [
-            jnp.sum(jnp.where(slot_of // each == w, lane << (slot_of % each * digits), 0))
-            for w in range(-(-listed.shape[1] // each))
-        ]
+        for w in range(words_ref.shape[0]):
+            word = jnp.where(slot_of // each == w, lane << (slot_of % each * digits), 0)
+            words_ref[w:w + 1] = jnp.broadcast_to(jnp.sum(word, axis=1, keepdims=True), (1, words_ref.shape[1]))
+    elif stage == "last":
+        words = [jnp.max(plan_ref[w:w + 1, :1]) for w in range(plan_ref.shape[0])]
 
     def place(slot, date):
         if stage == "last":
@@ -183,8 +183,16 @@
         last, first = edge[:, :, :half], edge[:, :, half:]
         return lax.ppermute(jnp.where(odd, last, first), "row", far)
 
+    def across(edge, flip):
+        last, first = edge[:, :, :half], edge[:, :, half:]
+        pairs = [((d ^ flip) * n_rows + j, d * n_rows + i) for d in range(size) for i, j in far]
+        return lax.ppermute(jnp.where(odd, last, first), ("date", "row"), pairs)
+
     def z(array, flip):
         return lax.ppermute(array, "date", pairs_of(size, flip))
+
+    def after(array, *others):
+        return lax.optimization_barrier((array,) + others)[0]
 
     def after(array, *others):
         return lax.optimization_barrier((array,) + others)[0]
@@ -200,6 +208,7 @@
     power_shape = (nd, rows, cols)
     vmem = pl.BlockSpec(memory_space=pltpu.VMEM)
     listed = jnp.maximum(plan, 0).reshape(1, -1)
+    digits = max(1, (size * nd - 1).bit_length())
     hbm = pl.BlockSpec(memory_space=pl.ANY)
 
     def scratch(total, slots):
@@ -217,33 +226,35 @@
     edge, inner = cut(stack_data)
     if size == 4:
         edge_2 = z(edge, 2)
+        inner_2 = z(inner, 2)
         edge_1 = z(edge, 1)
-        inner_2 = z(inner, 2)
         inner_1 = z(inner, 1)
         edge_3 = z(edge_2, 1)
         inner_3 = z(inner_2, 1)
         early = join(edge, edge_1, edge_2)
-        near_a, far_a = rim_near(early), rim_far(early)
-        near_b, far_b = rim_near(edge_3), rim_far(edge_3)
+        far_a = rim_far(early)
+        far_b = across(edge_2, 1)
+        near_a, near_b = rim_near(early), rim_near(after(edge_3, inner_1))
         slots = 3 * nd
-        operands = [edge, edge_1, edge_2, inner, inner_1, inner_2, far_a, near_a, band]
-        own, power, done = pl.pallas_call(
-            functools.partial(kernel, ([nd] * 3, [slots], [slots]), nd, 0, "early", n_rows),
+        operands = [listed, edge, edge_1, edge_2, inner, inner_1, inner_2, near_a, far_a, band]
+        own, power, done, words = pl.pallas_call(
+            functools.partial(kernel, ([nd] * 3, [slots], [slots]), nd, 0, "early", n_rows, digits),
             out_shape=[
                 jax.ShapeDtypeStruct(own_shape, jnp.float32),
                 jax.ShapeDtypeStruct(power_shape, jnp.float32),
                 jax.ShapeDtypeStruct((nd, slots, 2, rows, cols), jnp.float32),
+                jax.ShapeDtypeStruct((-(-size * nd // (31 // digits)), 128), jnp.int32),
             ],
             in_specs=[vmem] * len(operands),
-            out_specs=[vmem] * 3,
+            out_specs=[vmem] * 4,
             scratch_shapes=scratch(slots, slots)[:2],
             compiler_params=params,
             cost_estimate=work(slots),
             name="early_dates",
         )(*operands)
-        operands = [listed, own, power, done, edge_3, inner_3, far_b, near_b, band]
+        operands = [words, own, power, done, edge_3, inner_3, near_b, far_b, band]
         return pl.pallas_call(
-            functools.partial(kernel, ([nd], [nd], [nd]), nd, slots, "last", n_rows),
+            functools.partial(kernel, ([nd], [nd], [nd]), nd, slots, "last", n_rows, digits),
             out_shape=out_shape,
             in_specs=[vmem] * len(operands),
             out_specs=hbm,
@@ -255,7 +266,7 @@
 
     gathered = lax.all_gather(stack_data, "date", axis=0, tiled=True)
     all_edge, all_inner = cut(gathered)
-    operands = [edge, all_edge, inner, all_inner, rim_far(edge), rim_far(all_edge), rim_near(edge), rim_near(all_edge)]
+    operands = [edge, all_edge, inner, all_inner, rim_near(edge), rim_near(all_edge), rim_far(edge), rim_far(all_edge)]
     slots = next(n for n in (8, 4, 2, 1) if (size * nd) % n == 0)
 
     def spec(array, chunk):
@@ -264,7 +275,7 @@
         return pl.BlockSpec(array.shape, lambda g: (0,) * array.ndim)
 
     return pl.pallas_call(
-        functools.partial(kernel, ([nd, slots],) * 3, nd, 0, "all", n_rows),
+        functools.partial(kernel, ([nd, slots],) * 3, nd, 0, "all", n_rows, digits),
         grid=(size * nd // slots,),
         out_shape=out_shape,
         in_specs=[vmem] + [spec(a, n % 2) for n, a in enumerate(operands)] + [spec(band, 0)],

time: 18.8 us -> 18.5 us (0.984)
  starting transfers between devices: 12.6 us -> 11.8 us
  waiting for transfers between devices: 1.73 us -> 2.47 us
    ppermute x2 -> x1, starting transfers between devices: 3.21 us -> 1.17 us  [rim_far(): return lax.ppermute(jnp.where(odd, last, first), 'row', far)]
    ppermute x0 -> x1, starting transfers between devices: none -> 1.06 us  [across(): return lax.ppermute(jnp.where(odd, last, first), ('date', 'row'), pairs)]
    ppermute x2, starting transfers between devices: 0.14 us -> 1.1 us  [rim_near(): return lax.ppermute(jnp.where(odd, first, last), 'row', near)]
    ppermute x6, starting transfers between devices: 9.22 us -> 8.45 us  [z(): return lax.ppermute(array, 'date', pairs_of(size, flip))]
    ppermute x6, waiting for transfers between devices: 1.46 us -> 2.17 us  [z(): return lax.ppermute(array, 'date', pairs_of(size, flip))]
  transfers between devices with their start and end apart: 10 -> 10, of which waited for: 6 -> 5; matrix products, arithmetic and copies ran while one was open for 1% -> 1% of each run, Pallas kernels for 5% -> 5%
where the time goes in v4:
time: 18.5 us; the launch traced here: 18.4 us
  starting transfers between devices  11.8 us (64%)
  waiting for transfers between devices  2.47 us (13%)
  Pallas kernels  2.31 us (12%)
  local copies, waits for them, and re-layouts  1.6 us (9%)
    ppermute x6, starting transfers between devices, z(): return lax.ppermute(array, 'date', pairs_of(size, flip))  8.45 us
    ppermute x6, waiting for transfers between devices, z(): return lax.ppermute(array, 'date', pairs_of(size, flip))  2.17 us
    pallas_call x1, Pallas kernels, body(): pl.pallas_call(functools.partial(kernel, ([nd], [nd], [nd]), nd, slots, '...  1.4 us
    ppermute x1, starting transfers between devices, rim_far(): return lax.ppermute(jnp.where(odd, last, first), 'row', far)  1.17 us
    ppermute x2, starting transfers between devices, rim_near(): return lax.ppermute(jnp.where(odd, first, last), 'row', near)  1.1 us
    ppermute x1, starting transfers between devices, across(): return lax.ppermute(jnp.where(odd, last, first), ('date', 'row'), pairs)  1.06 us
    slice x1, local copies, waits for them, and re-layouts, cut(): first, last = (block[:, :, :half], block[:, :, rows - half:])  0.93 us
    pallas_call x1, Pallas kernels, body(): pl.pallas_call(functools.partial(kernel, ([nd] * 3, [slots], [slots]), nd...  0.92 us
  transfers between devices with their start and end apart: 10, of which 5 were waited for; matrix products, arithmetic and copies ran while one was open for 1% of the time, Pallas kernels for 5%

profile of v4, /device:TPU:0, one launch (start us, length us, event | category | flops | bytes accessed | tf_op | source)
XLA Modules:
  0.0 18.4 jit_solution(7325152517166646909)
XLA Ops:
  0.0 0.0 copy-start
  0.0 0.9 %fusion.1 = (f32[2,2,4,512]{3,2,1,0:T(4,128)S(1)}, f32[2,2,4,512]{3,2,1,0:T(4,128)S(1)}) fusion(f32[2,2,16,512]{3,2,1,0:T(8,128)} %param.2), kind=kLoop, calls=%fused_computation.9 | loop fusion | bytes 131072 | tf_op jit(solution)/shard_map/slice | solution.py:175
  1.0 4.1 %collective-permute-start.1 = (f32[2,2,8,512]{3,2,1,0:T(8,128)S(1)}, f32[2,2,8,512]{3,2,1,0:T(8,128)S(1)}, u32[]{:S(2)}, u32[]{:S(2)}) collective-permute-start(f32[2,2,8,512]{3,2,1,0:T(8,128)S(1)} %pad_maximum_fusion.1.refs_1_), channel_id=1, source_target_pairs={{0,8},{4,12},{8,0},{12,4},{1,9},{5,13},{9,1},{13,5},{2,10},{6,14},... | collective-permute-start | bytes 196616 | tf_op jit(solution)/shard_map/ppermute | solution.py:192
  5.1 1.6 %collective-permute-start = (f32[2,2,8,512]{3,2,1,0:T(8,128)S(1)}, f32[2,2,8,512]{3,2,1,0:T(8,128)S(1)}, u32[]{:S(2)}, u32[]{:S(2)}) collective-permute-start(f32[2,2,8,512]{3,2,1,0:T(8,128)S(1)} %pad_maximum_fusion.1.refs_1_), channel_id=1, source_target_pairs={{0,4},{4,0},{8,12},{12,8},{1,5},{5,1},{9,13},{13,9},{2,6},{6,2},{1... | collective-permute-start | bytes 196616 | tf_op jit(solution)/shard_map/ppermute | solution.py:192
  6.6 0.0 copy-done
  6.7 0.4 %collective-permute-start.3 = (f32[2,2,8,512]{3,2,1,0:T(8,128)S(1)}, f32[2,2,8,512]{3,2,1,0:T(8,128)S(1)}, u32[]{:S(2)}, u32[]{:S(2)}) collective-permute-start(f32[2,2,8,512]{3,2,1,0:T(8,128)S(1)} %slice.31.refs_4_), channel_id=1, source_target_pairs={{0,8},{4,12},{8,0},{12,4},{1,9},{5,13},{9,1},{13,5},{2,10},{6,14},... | collective-permute-start | bytes 196616 | tf_op jit(solution)/shard_map/ppermute | solution.py:192
  7.1 0.2 %collective-permute-start.2 = (f32[2,2,8,512]{3,2,1,0:T(8,128)S(1)}, f32[2,2,8,512]{3,2,1,0:T(8,128)S(1)}, u32[]{:S(2)}, u32[]{:S(2)}) collective-permute-start(f32[2,2,8,512]{3,2,1,0:T(8,128)S(1)} %slice.31.refs_4_), channel_id=1, source_target_pairs={{0,4},{4,0},{8,12},{12,8},{1,5},{5,1},{9,13},{13,9},{2,6},{6,2},{1... | collective-permute-start | bytes 196616 | tf_op jit(solution)/shard_map/ppermute | solution.py:192
  7.2 0.0 copy-start.1
  7.3 0.7 %copy-done.1 = s32[8]{0:T(128)S(1)} copy-done((s32[8]{0:T(128)S(1)}, s32[8]{0:T(128)}, u32[]{:S(2)}) %copy-start.1) | copy-done | bytes 56
  7.9 0.1 fusion.refs_9_.refs_8_
  8.0 0.1 collective-permute-done.1.refs_3_
  8.1 1.1 %collective-permute-start.9 = (f32[2,2,4,512]{3,2,1,0:T(4,128)S(1)}, f32[2,2,4,512]{3,2,1,0:T(4,128)S(1)}, u32[]{:S(2)}, u32[]{:S(2)}) collective-permute-start(f32[2,2,4,512]{3,2,1,0:T(4,128)S(1)} %slice_select_fusion.2), channel_id=1, source_target_pairs={{6,1},{4,3},{5,2},{7,0},{2,5},{0,7},{1,6},{3,4},{14,9},{12,11},{13... | collective-permute-start | bytes 98312 | tf_op jit(solution)/shard_map/ppermute | solution.py:189
  9.2 1.1 %collective-permute-start.6 = (f32[2,2,8,512]{3,2,1,0:T(8,128)S(1)}, f32[2,2,8,512]{3,2,1,0:T(8,128)S(1)}, u32[]{:S(2)}, u32[]{:S(2)}) collective-permute-start(f32[2,2,8,512]{3,2,1,0:T(8,128)S(1)} %collective-permute-done.1.refs_3_), channel_id=1, source_target_pairs={{0,4},{4,0},{8,12},{12,8},{1,5},{5,1},{9,13},{13,9},{2,6},{6,2},{1... | collective-permute-start | bytes 196616 | tf_op jit(solution)/shard_map/ppermute | solution.py:192
  10.3 0.0 collective-permute-done.refs_2_
  10.4 1.2 %collective-permute-start.5 = (f32[6,2,4,512]{3,2,1,0:T(4,128)S(1)}, f32[6,2,4,512]{3,2,1,0:T(4,128)S(1)}, u32[]{:S(2)}, u32[]{:S(2)}) collective-permute-start(f32[6,2,4,512]{3,2,1,0:T(4,128)S(1)} %get-tuple-element.15), channel_id=1, source_target_pairs={{1,2},{3,0},{2,1},{0,3},{5,6},{7,4},{6,5},{4,7},{9,10},{11,8},{10,... | collective-permute-start | bytes 294920 | tf_op jit(solution)/shard_map/ppermute | solution.py:184
  11.6 0.9 %collective-permute-done.3.refs_6_ = f32[2,2,8,512]{3,2,1,0:T(8,128)S(1)} collective-permute-done((f32[2,2,8,512]{3,2,1,0:T(8,128)S(1)}, f32[2,2,8,512]{3,2,1,0:T(8,128)S(1)}, u32[]{:S(2)}, u32[]{:S(2)}) %collective-permute-start.3) | collective-permute-done | bytes 65568 | tf_op jit(solution)/shard_map/ppermute | solution.py:192
  12.5 0.0 collective-permute-start.4
  12.5 0.0 collective-permute-done.2.refs_5_
  12.5 1.0 %collective-permute-start.7 = (f32[2,2,8,512]{3,2,1,0:T(8,128)S(1)}, f32[2,2,8,512]{3,2,1,0:T(8,128)S(1)}, u32[]{:S(2)}, u32[]{:S(2)}) collective-permute-start(f32[2,2,8,512]{3,2,1,0:T(8,128)S(1)} %collective-permute-done.3.refs_6_), channel_id=1, source_target_pairs={{0,4},{4,0},{8,12},{12,8},{1,5},{5,1},{9,13},{13,9},{2,6},{6,2},{1... | collective-permute-start | bytes 196616 | tf_op jit(solution)/shard_map/ppermute | solution.py:192
  13.5 0.1 collective-permute-done.6.refs_4_
  13.7 1.1 %collective-permute-start.8 = (f32[2,2,4,512]{3,2,1,0:T(4,128)S(1)}, f32[2,2,4,512]{3,2,1,0:T(4,128)S(1)}, u32[]{:S(2)}, u32[]{:S(2)}) collective-permute-start(f32[2,2,4,512]{3,2,1,0:T(4,128)S(1)} %slice_select_fusion.3), channel_id=1, source_target_pairs={{0,1},{1,0},{2,3},{3,2},{4,5},{5,4},{6,7},{7,6},{8,9},{9,8},{10,11... | collective-permute-start | bytes 98312 | tf_op jit(solution)/shard_map/ppermute | solution.py:180
  14.8 0.3 %collective-permute-done.5.refs_8_ = f32[6,2,4,512]{3,2,1,0:T(4,128)S(1)} collective-permute-done((f32[6,2,4,512]{3,2,1,0:T(4,128)S(1)}, f32[6,2,4,512]{3,2,1,0:T(4,128)S(1)}, u32[]{:S(2)}, u32[]{:S(2)}) %collective-permute-start.5) | collective-permute-done | bytes 98336 | tf_op jit(solution)/shard_map/ppermute | solution.py:184
  15.1 0.0 collective-permute-done.4.refs_7_
  15.1 0.9 %early_dates.1 = (f32[2,2,24,512]{3,2,1,0:T(8,128)S(1)}, f32[2,16,512]{2,1,0:T(8,128)S(1)}, f32[2,6,2,16,512]{4,3,2,1,0:T(8,128)S(1)}, s32[1,128]{1,0:T(1,128)S(1)}) custom-call(s32[1,8]{1,0:T(1,128)S(1)} %maximum_bitcast_fusion.refs_0_, f32[2,2,8,512]{3,2,1,0:T(8,128)S(1)} %pad_maximum_fusion.1.refs_1_, f32[2,2,8,512]{3,2,1,0:T(8,128)S(1)} %collective-permute-done.refs_2_, ...), custom_call_target="tpu_custom_call" | custom-call | flops 805306368 | bytes 1572864 | tf_op jit(solution)/shard_map/early_dates/pallas_call | solution.py:240
  16.0 0.0 collective-permute-done.9.refs_7_
  16.0 1.0 %collective-permute-done.7.refs_5_ = f32[2,2,8,512]{3,2,1,0:T(8,128)S(1)} collective-permute-done((f32[2,2,8,512]{3,2,1,0:T(8,128)S(1)}, f32[2,2,8,512]{3,2,1,0:T(8,128)S(1)}, u32[]{:S(2)}, u32[]{:S(2)}) %collective-permute-start.7) | collective-permute-done | bytes 65568 | tf_op jit(solution)/shard_map/ppermute | solution.py:192
  17.0 0.0 collective-permute-done.8.refs_6_
  17.0 1.4 %last_dates.1 = f32[2,8,2,16,512]{4,3,2,1,0:T(8,128)} custom-call(s32[1,128]{1,0:T(1,128)S(1)} %get-tuple-element.10.refs_0_, f32[2,2,24,512]{3,2,1,0:T(8,128)S(1)} %get-tuple-element.11.refs_1_, f32[2,16,512]{2,1,0:T(8,128)S(1)} %get-tuple-element.12.refs_2_, f32[2,6,2,16,512]{4,3,2,1,0:T(8,128)S(1)} %get-tuple-element.13.refs_3_, ...), custom_call_target="tpu_custom_call" | custom-call | flops 268435456 | bytes 524288 | tf_op jit(solution)/shard_map/last_dates/pallas_call | solution.py:256
  (7 shorter events, 0.1 us)
Async XLA Ops:
  0.0 6.6 %copy-start = (f32[2,2,16,512]{3,2,1,0:T(8,128)S(1)}, f32[2,2,16,512]{3,2,1,0:T(8,128)}, u32[]{:S(2)}) copy-start(f32[2,2,16,512]{3,2,1,0:T(8,128)} %param.2) | copy-start | bytes 393220
  1.0 7.2 %collective-permute-start.1 = (f32[2,2,8,512]{3,2,1,0:T(8,128)S(1)}, f32[2,2,8,512]{3,2,1,0:T(8,128)S(1)}, u32[]{:S(2)}, u32[]{:S(2)}) collective-permute-start(f32[2,2,8,512]{3,2,1,0:T(8,128)S(1)} %pad_maximum_fusion.1.refs_1_), channel_id=1, source_target_pairs={{0,8},{4,12},{8,0},{12,4},{1,9},{5,13},{9,1},{13,5},{2,10},{6,14},... | collective-permute-start | bytes 196616 | tf_op jit(solution)/shard_map/ppermute | solution.py:192
  5.1 5.3 %collective-permute-start = (f32[2,2,8,512]{3,2,1,0:T(8,128)S(1)}, f32[2,2,8,512]{3,2,1,0:T(8,128)S(1)}, u32[]{:S(2)}, u32[]{:S(2)}) collective-permute-start(f32[2,2,8,512]{3,2,1,0:T(8,128)S(1)} %pad_maximum_fusion.1.refs_1_), channel_id=1, source_target_pairs={{0,4},{4,0},{8,12},{12,8},{1,5},{5,1},{9,13},{13,9},{2,6},{6,2},{1... | collective-permute-start | bytes 196616 | tf_op jit(solution)/shard_map/ppermute | solution.py:192
  6.7 5.8 %collective-permute-start.3 = (f32[2,2,8,512]{3,2,1,0:T(8,128)S(1)}, f32[2,2,8,512]{3,2,1,0:T(8,128)S(1)}, u32[]{:S(2)}, u32[]{:S(2)}) collective-permute-start(f32[2,2,8,512]{3,2,1,0:T(8,128)S(1)} %slice.31.refs_4_), channel_id=1, source_target_pairs={{0,8},{4,12},{8,0},{12,4},{1,9},{5,13},{9,1},{13,5},{2,10},{6,14},... | collective-permute-start | bytes 196616 | tf_op jit(solution)/shard_map/ppermute | solution.py:192
  7.1 5.4 %collective-permute-start.2 = (f32[2,2,8,512]{3,2,1,0:T(8,128)S(1)}, f32[2,2,8,512]{3,2,1,0:T(8,128)S(1)}, u32[]{:S(2)}, u32[]{:S(2)}) collective-permute-start(f32[2,2,8,512]{3,2,1,0:T(8,128)S(1)} %slice.31.refs_4_), channel_id=1, source_target_pairs={{0,4},{4,0},{8,12},{12,8},{1,5},{5,1},{9,13},{13,9},{2,6},{6,2},{1... | collective-permute-start | bytes 196616 | tf_op jit(solution)/shard_map/ppermute | solution.py:192
  7.2 0.7 %copy-start.1 = (s32[8]{0:T(128)S(1)}, s32[8]{0:T(128)}, u32[]{:S(2)}) copy-start(s32[8]{0:T(128)} %param.3) | copy-start | bytes 100
  8.1 7.9 %collective-permute-start.9 = (f32[2,2,4,512]{3,2,1,0:T(4,128)S(1)}, f32[2,2,4,512]{3,2,1,0:T(4,128)S(1)}, u32[]{:S(2)}, u32[]{:S(2)}) collective-permute-start(f32[2,2,4,512]{3,2,1,0:T(4,128)S(1)} %slice_select_fusion.2), channel_id=1, source_target_pairs={{6,1},{4,3},{5,2},{7,0},{2,5},{0,7},{1,6},{3,4},{14,9},{12,11},{13... | collective-permute-start | bytes 98312 | tf_op jit(solution)/shard_map/ppermute | solution.py:189
  9.2 4.5 %collective-permute-start.6 = (f32[2,2,8,512]{3,2,1,0:T(8,128)S(1)}, f32[2,2,8,512]{3,2,1,0:T(8,128)S(1)}, u32[]{:S(2)}, u32[]{:S(2)}) collective-permute-start(f32[2,2,8,512]{3,2,1,0:T(8,128)S(1)} %collective-permute-done.1.refs_3_), channel_id=1, source_target_pairs={{0,4},{4,0},{8,12},{12,8},{1,5},{5,1},{9,13},{13,9},{2,6},{6,2},{1... | collective-permute-start | bytes 196616 | tf_op jit(solution)/shard_map/ppermute | solution.py:192
  10.4 4.7 %collective-permute-start.5 = (f32[6,2,4,512]{3,2,1,0:T(4,128)S(1)}, f32[6,2,4,512]{3,2,1,0:T(4,128)S(1)}, u32[]{:S(2)}, u32[]{:S(2)}) collective-permute-start(f32[6,2,4,512]{3,2,1,0:T(4,128)S(1)} %get-tuple-element.15), channel_id=1, source_target_pairs={{1,2},{3,0},{2,1},{0,3},{5,6},{7,4},{6,5},{4,7},{9,10},{11,8},{10,... | collective-permute-start | bytes 294920 | tf_op jit(solution)/shard_map/ppermute | solution.py:184
  12.5 2.6 %collective-permute-start.4 = (f32[6,2,4,512]{3,2,1,0:T(4,128)S(1)}, f32[6,2,4,512]{3,2,1,0:T(4,128)S(1)}, u32[]{:S(2)}, u32[]{:S(2)}) collective-permute-start(f32[6,2,4,512]{3,2,1,0:T(4,128)S(1)} %get-tuple-element.16), channel_id=1, source_target_pairs={{0,1},{1,0},{2,3},{3,2},{4,5},{5,4},{6,7},{7,6},{8,9},{9,8},{10,11... | collective-permute-start | bytes 294920 | tf_op jit(solution)/shard_map/ppermute | solution.py:180
  12.5 4.5 %collective-permute-start.7 = (f32[2,2,8,512]{3,2,1,0:T(8,128)S(1)}, f32[2,2,8,512]{3,2,1,0:T(8,128)S(1)}, u32[]{:S(2)}, u32[]{:S(2)}) collective-permute-start(f32[2,2,8,512]{3,2,1,0:T(8,128)S(1)} %collective-permute-done.3.refs_6_), channel_id=1, source_target_pairs={{0,4},{4,0},{8,12},{12,8},{1,5},{5,1},{9,13},{13,9},{2,6},{6,2},{1... | collective-permute-start | bytes 196616 | tf_op jit(solution)/shard_map/ppermute | solution.py:192
  13.7 3.3 %collective-permute-start.8 = (f32[2,2,4,512]{3,2,1,0:T(4,128)S(1)}, f32[2,2,4,512]{3,2,1,0:T(4,128)S(1)}, u32[]{:S(2)}, u32[]{:S(2)}) collective-permute-start(f32[2,2,4,512]{3,2,1,0:T(4,128)S(1)} %slice_select_fusion.3), channel_id=1, source_target_pairs={{0,1},{1,0},{2,3},{3,2},{4,5},{5,4},{6,7},{7,6},{8,9},{9,8},{10,11... | collective-permute-start | bytes 98312 | tf_op jit(solution)/shard_map/ppermute | solution.py:180

commit v5 on v4

--- a/solution.py
+++ b/solution.py
@@ -9,6 +9,7 @@
 
 HALF_ROWS = 4
 HALF_COLS = 16
+LANES = 128
 epsilon = 1e-06
 
 
@@ -75,10 +76,9 @@
         else:
             date = (lax.axis_index("date") ^ (slot // nd)) * nd + slot % nd
         k = place(slot, date)
-        for d in range(nd):
-            copy = pltpu.make_async_copy(ref[d], out_ref.at[d, k], sems.at[d, slot])
-            copy.start()
-            copies.append(copy)
+        copy = pltpu.make_async_copy(ref, out_ref.at[:, k], sems.at[slot])
+        copy.start()
+        copies.append(copy)
 
     at = 0
     for ref, inner, count in zip(edges, inners, counts[0]):
@@ -102,9 +102,18 @@
     def columns(fields):
         high, low = zip(*(split(f) for f in fields))
         both = jnp.concatenate(high + low, axis=0)
-        out = jnp.dot(both, band, preferred_element_type=jnp.float32)
-        middle = out.shape[0] // 2
-        return out[:middle] + out[middle:]
+        tiles = both.shape[1] // LANES
+        height = both.shape[0] // 2
+        lane = lax.broadcasted_iota(jnp.int32, (height, LANES), 1)
+        parts = []
+        for t in range(tiles - 1):
+            out = jnp.dot(both[:, t * LANES:(t + 2) * LANES], band, preferred_element_type=jnp.float32)
+            parts.append(out[:height] + out[height:])
+        sums = [parts[0][:, :LANES]]
+        for t in range(1, tiles - 1):
+            sums.append(jnp.where(lane < LANES // 2, parts[t - 1][:, LANES:], parts[t][:, :LANES]))
+        sums.append(parts[-1][:, LANES:])
+        return jnp.concatenate(sums, axis=1)
 
     def power_of(re, im):
         return row_window(re * re + im * im, rows)
@@ -149,9 +158,9 @@
             buf[d, s, 1] = res[s, at + rows:at + 2 * rows] * factor
         if stage == "last" and s == 0:
             for t in range(own):
-                send([done.at[d, t] for d in range(nd)], t)
+                send(done.at[:, t], t)
         if stage != "early":
-            send([buf.at[d, s] for d in range(nd)], own + s)
+            send(buf.at[:, s], own + s)
     for copy in copies:
         copy.wait()
 
@@ -200,8 +209,8 @@
     def join(*blocks):
         return jnp.concatenate(blocks, axis=0)
 
-    out_col = lax.broadcasted_iota(jnp.int32, (cols, cols), 0)
-    in_col = lax.broadcasted_iota(jnp.int32, (cols, cols), 1)
+    out_col = lax.broadcasted_iota(jnp.int32, (2 * LANES, 2 * LANES), 0)
+    in_col = lax.broadcasted_iota(jnp.int32, (2 * LANES, 2 * LANES), 1)
     band = (jnp.abs(out_col - in_col) <= HALF_COLS).astype(jnp.bfloat16)
     out_shape = jax.ShapeDtypeStruct((nd, size * nd, 2, rows, cols), jnp.float32)
     own_shape = (nd, 2, rows + 2 * half, cols)
@@ -258,7 +267,7 @@
             out_shape=out_shape,
             in_specs=[vmem] * len(operands),
             out_specs=hbm,
-            scratch_shapes=scratch(nd, nd) + [pltpu.SemaphoreType.DMA((nd, size * nd))],
+            scratch_shapes=scratch(nd, nd) + [pltpu.SemaphoreType.DMA((size * nd,))],
             compiler_params=params,
             cost_estimate=work(nd),
             name="last_dates",
@@ -284,7 +293,7 @@
         + [
             pltpu.VMEM(own_shape, jnp.float32),
             pltpu.VMEM(power_shape, jnp.float32),
-            pltpu.SemaphoreType.DMA((nd, slots)),
+            pltpu.SemaphoreType.DMA((slots,)),
         ],
         compiler_params=params,
         name="all_dates",

time: 18.5 us -> 18.4 us (level)
  no operation moved by 1% of the time
where the time goes in v5:
time: 18.4 us; the launch traced here: 18.3 us
  starting transfers between devices  11.8 us (64%)
  waiting for transfers between devices  2.56 us (14%)
  Pallas kernels  2.15 us (12%)
  local copies, waits for them, and re-layouts  1.6 us (9%)
    ppermute x6, starting transfers between devices, z(): return lax.ppermute(array, 'date', pairs_of(size, flip))  8.49 us
    ppermute x6, waiting for transfers between devices, z(): return lax.ppermute(array, 'date', pairs_of(size, flip))  2.26 us
    pallas_call x1, Pallas kernels, body(): pl.pallas_call(functools.partial(kernel, ([nd], [nd], [nd]), nd, slots, '...  1.29 us
    ppermute x1, starting transfers between devices, rim_far(): return lax.ppermute(jnp.where(odd, last, first), 'row', far)  1.17 us
    ppermute x2, starting transfers between devices, rim_near(): return lax.ppermute(jnp.where(odd, first, last), 'row', near)  1.1 us
    ppermute x1, starting transfers between devices, across(): return lax.ppermute(jnp.where(odd, last, first), ('date', 'row'), pairs)  1.02 us
    slice x1, local copies, waits for them, and re-layouts, cut(): first, last = (block[:, :, :half], block[:, :, rows - half:])  0.93 us
    pallas_call x1, Pallas kernels, body(): pl.pallas_call(functools.partial(kernel, ([nd] * 3, [slots], [slots]), nd...  0.86 us
  transfers between devices with their start and end apart: 10, of which 5 were waited for; matrix products, arithmetic and copies ran while one was open for 1% of the time, Pallas kernels for 5%

profile of v5, /device:TPU:0, one launch (start us, length us, event | category | flops | bytes accessed | tf_op | source)
XLA Modules:
  0.0 18.3 jit_solution(1114760897723434751)
XLA Ops:
  0.0 0.0 copy-start
  0.0 0.9 %fusion.1 = (f32[2,2,4,512]{3,2,1,0:T(4,128)S(1)}, f32[2,2,4,512]{3,2,1,0:T(4,128)S(1)}) fusion(f32[2,2,16,512]{3,2,1,0:T(8,128)} %param.2), kind=kLoop, calls=%fused_computation.9 | loop fusion | bytes 131072 | tf_op jit(solution)/shard_map/slice | solution.py:184
  1.0 4.1 %collective-permute-start.1 = (f32[2,2,8,512]{3,2,1,0:T(8,128)S(1)}, f32[2,2,8,512]{3,2,1,0:T(8,128)S(1)}, u32[]{:S(2)}, u32[]{:S(2)}) collective-permute-start(f32[2,2,8,512]{3,2,1,0:T(8,128)S(1)} %pad_maximum_fusion.1.refs_1_), channel_id=1, source_target_pairs={{0,8},{4,12},{8,0},{12,4},{1,9},{5,13},{9,1},{13,5},{2,10},{6,14},... | collective-permute-start | bytes 196616 | tf_op jit(solution)/shard_map/ppermute | solution.py:201
  5.1 1.6 %collective-permute-start = (f32[2,2,8,512]{3,2,1,0:T(8,128)S(1)}, f32[2,2,8,512]{3,2,1,0:T(8,128)S(1)}, u32[]{:S(2)}, u32[]{:S(2)}) collective-permute-start(f32[2,2,8,512]{3,2,1,0:T(8,128)S(1)} %pad_maximum_fusion.1.refs_1_), channel_id=1, source_target_pairs={{0,4},{4,0},{8,12},{12,8},{1,5},{5,1},{9,13},{13,9},{2,6},{6,2},{1... | collective-permute-start | bytes 196616 | tf_op jit(solution)/shard_map/ppermute | solution.py:201
  6.6 0.0 copy-done
  6.7 0.4 %collective-permute-start.3 = (f32[2,2,8,512]{3,2,1,0:T(8,128)S(1)}, f32[2,2,8,512]{3,2,1,0:T(8,128)S(1)}, u32[]{:S(2)}, u32[]{:S(2)}) collective-permute-start(f32[2,2,8,512]{3,2,1,0:T(8,128)S(1)} %slice.31.refs_4_), channel_id=1, source_target_pairs={{0,8},{4,12},{8,0},{12,4},{1,9},{5,13},{9,1},{13,5},{2,10},{6,14},... | collective-permute-start | bytes 196616 | tf_op jit(solution)/shard_map/ppermute | solution.py:201
  7.1 0.2 %collective-permute-start.2 = (f32[2,2,8,512]{3,2,1,0:T(8,128)S(1)}, f32[2,2,8,512]{3,2,1,0:T(8,128)S(1)}, u32[]{:S(2)}, u32[]{:S(2)}) collective-permute-start(f32[2,2,8,512]{3,2,1,0:T(8,128)S(1)} %slice.31.refs_4_), channel_id=1, source_target_pairs={{0,4},{4,0},{8,12},{12,8},{1,5},{5,1},{9,13},{13,9},{2,6},{6,2},{1... | collective-permute-start | bytes 196616 | tf_op jit(solution)/shard_map/ppermute | solution.py:201
  7.2 0.0 copy-start.1
  7.3 0.7 %copy-done.1 = s32[8]{0:T(128)S(1)} copy-done((s32[8]{0:T(128)S(1)}, s32[8]{0:T(128)}, u32[]{:S(2)}) %copy-start.1) | copy-done | bytes 56
  8.0 0.2 collective-permute-done.1.refs_3_
  8.1 1.0 %collective-permute-start.9 = (f32[2,2,4,512]{3,2,1,0:T(4,128)S(1)}, f32[2,2,4,512]{3,2,1,0:T(4,128)S(1)}, u32[]{:S(2)}, u32[]{:S(2)}) collective-permute-start(f32[2,2,4,512]{3,2,1,0:T(4,128)S(1)} %slice_select_fusion.2), channel_id=1, source_target_pairs={{6,1},{4,3},{5,2},{7,0},{2,5},{0,7},{1,6},{3,4},{14,9},{12,11},{13... | collective-permute-start | bytes 98312 | tf_op jit(solution)/shard_map/ppermute | solution.py:198
  9.2 1.2 %collective-permute-start.6 = (f32[2,2,8,512]{3,2,1,0:T(8,128)S(1)}, f32[2,2,8,512]{3,2,1,0:T(8,128)S(1)}, u32[]{:S(2)}, u32[]{:S(2)}) collective-permute-start(f32[2,2,8,512]{3,2,1,0:T(8,128)S(1)} %collective-permute-done.1.refs_3_), channel_id=1, source_target_pairs={{0,4},{4,0},{8,12},{12,8},{1,5},{5,1},{9,13},{13,9},{2,6},{6,2},{1... | collective-permute-start | bytes 196616 | tf_op jit(solution)/shard_map/ppermute | solution.py:201
  10.3 0.0 collective-permute-done.refs_2_
  10.4 1.2 %collective-permute-start.5 = (f32[6,2,4,512]{3,2,1,0:T(4,128)S(1)}, f32[6,2,4,512]{3,2,1,0:T(4,128)S(1)}, u32[]{:S(2)}, u32[]{:S(2)}) collective-permute-start(f32[6,2,4,512]{3,2,1,0:T(4,128)S(1)} %get-tuple-element.15), channel_id=1, source_target_pairs={{1,2},{3,0},{2,1},{0,3},{5,6},{7,4},{6,5},{4,7},{9,10},{11,8},{10,... | collective-permute-start | bytes 294920 | tf_op jit(solution)/shard_map/ppermute | solution.py:193
  11.6 0.9 %collective-permute-done.3.refs_6_ = f32[2,2,8,512]{3,2,1,0:T(8,128)S(1)} collective-permute-done((f32[2,2,8,512]{3,2,1,0:T(8,128)S(1)}, f32[2,2,8,512]{3,2,1,0:T(8,128)S(1)}, u32[]{:S(2)}, u32[]{:S(2)}) %collective-permute-start.3) | collective-permute-done | bytes 65568 | tf_op jit(solution)/shard_map/ppermute | solution.py:201
  12.5 0.0 collective-permute-start.4
  12.5 0.0 collective-permute-done.2.refs_5_
  12.5 1.0 %collective-permute-start.7 = (f32[2,2,8,512]{3,2,1,0:T(8,128)S(1)}, f32[2,2,8,512]{3,2,1,0:T(8,128)S(1)}, u32[]{:S(2)}, u32[]{:S(2)}) collective-permute-start(f32[2,2,8,512]{3,2,1,0:T(8,128)S(1)} %collective-permute-done.3.refs_6_), channel_id=1, source_target_pairs={{0,4},{4,0},{8,12},{12,8},{1,5},{5,1},{9,13},{13,9},{2,6},{6,2},{1... | collective-permute-start | bytes 196616 | tf_op jit(solution)/shard_map/ppermute | solution.py:201
  13.5 0.1 collective-permute-done.6.refs_4_
  13.7 1.1 %collective-permute-start.8 = (f32[2,2,4,512]{3,2,1,0:T(4,128)S(1)}, f32[2,2,4,512]{3,2,1,0:T(4,128)S(1)}, u32[]{:S(2)}, u32[]{:S(2)}) collective-permute-start(f32[2,2,4,512]{3,2,1,0:T(4,128)S(1)} %slice_select_fusion.3), channel_id=1, source_target_pairs={{0,1},{1,0},{2,3},{3,2},{4,5},{5,4},{6,7},{7,6},{8,9},{9,8},{10,11... | collective-permute-start | bytes 98312 | tf_op jit(solution)/shard_map/ppermute | solution.py:189
  14.8 0.3 %collective-permute-done.5.refs_8_ = f32[6,2,4,512]{3,2,1,0:T(4,128)S(1)} collective-permute-done((f32[6,2,4,512]{3,2,1,0:T(4,128)S(1)}, f32[6,2,4,512]{3,2,1,0:T(4,128)S(1)}, u32[]{:S(2)}, u32[]{:S(2)}) %collective-permute-start.5) | collective-permute-done | bytes 98336 | tf_op jit(solution)/shard_map/ppermute | solution.py:193
  15.1 0.0 collective-permute-done.4.refs_7_
  15.1 0.9 %early_dates.1 = (f32[2,2,24,512]{3,2,1,0:T(8,128)S(1)}, f32[2,16,512]{2,1,0:T(8,128)S(1)}, f32[2,6,2,16,512]{4,3,2,1,0:T(8,128)S(1)}, s32[1,128]{1,0:T(1,128)S(1)}) custom-call(s32[1,8]{1,0:T(1,128)S(1)} %maximum_bitcast_fusion.refs_0_, f32[2,2,8,512]{3,2,1,0:T(8,128)S(1)} %pad_maximum_fusion.1.refs_1_, f32[2,2,8,512]{3,2,1,0:T(8,128)S(1)} %collective-permute-done.refs_2_, ...), custom_call_target="tpu_custom_call" | custom-call | flops 805306368 | bytes 1572864 | tf_op jit(solution)/shard_map/early_dates/pallas_call | solution.py:249
  15.9 0.0 collective-permute-done.9.refs_7_
  16.0 1.0 %collective-permute-done.7.refs_5_ = f32[2,2,8,512]{3,2,1,0:T(8,128)S(1)} collective-permute-done((f32[2,2,8,512]{3,2,1,0:T(8,128)S(1)}, f32[2,2,8,512]{3,2,1,0:T(8,128)S(1)}, u32[]{:S(2)}, u32[]{:S(2)}) %collective-permute-start.7) | collective-permute-done | bytes 65568 | tf_op jit(solution)/shard_map/ppermute | solution.py:201
  17.0 0.0 collective-permute-done.8.refs_6_
  17.0 1.3 %last_dates.1 = f32[2,8,2,16,512]{4,3,2,1,0:T(8,128)} custom-call(s32[1,128]{1,0:T(1,128)S(1)} %get-tuple-element.10.refs_0_, f32[2,2,24,512]{3,2,1,0:T(8,128)S(1)} %get-tuple-element.11.refs_1_, f32[2,16,512]{2,1,0:T(8,128)S(1)} %get-tuple-element.12.refs_2_, f32[2,6,2,16,512]{4,3,2,1,0:T(8,128)S(1)} %get-tuple-element.13.refs_3_, ...), custom_call_target="tpu_custom_call" | custom-call | flops 268435456 | bytes 524288 | tf_op jit(solution)/shard_map/last_dates/pallas_call | solution.py:265
  (8 shorter events, 0.2 us)
Async XLA Ops:
  0.0 6.6 %copy-start = (f32[2,2,16,512]{3,2,1,0:T(8,128)S(1)}, f32[2,2,16,512]{3,2,1,0:T(8,128)}, u32[]{:S(2)}) copy-start(f32[2,2,16,512]{3,2,1,0:T(8,128)} %param.2) | copy-start | bytes 393220
  1.0 7.2 %collective-permute-start.1 = (f32[2,2,8,512]{3,2,1,0:T(8,128)S(1)}, f32[2,2,8,512]{3,2,1,0:T(8,128)S(1)}, u32[]{:S(2)}, u32[]{:S(2)}) collective-permute-start(f32[2,2,8,512]{3,2,1,0:T(8,128)S(1)} %pad_maximum_fusion.1.refs_1_), channel_id=1, source_target_pairs={{0,8},{4,12},{8,0},{12,4},{1,9},{5,13},{9,1},{13,5},{2,10},{6,14},... | collective-permute-start | bytes 196616 | tf_op jit(solution)/shard_map/ppermute | solution.py:201
  5.1 5.3 %collective-permute-start = (f32[2,2,8,512]{3,2,1,0:T(8,128)S(1)}, f32[2,2,8,512]{3,2,1,0:T(8,128)S(1)}, u32[]{:S(2)}, u32[]{:S(2)}) collective-permute-start(f32[2,2,8,512]{3,2,1,0:T(8,128)S(1)} %pad_maximum_fusion.1.refs_1_), channel_id=1, source_target_pairs={{0,4},{4,0},{8,12},{12,8},{1,5},{5,1},{9,13},{13,9},{2,6},{6,2},{1... | collective-permute-start | bytes 196616 | tf_op jit(solution)/shard_map/ppermute | solution.py:201
  6.7 5.8 %collective-permute-start.3 = (f32[2,2,8,512]{3,2,1,0:T(8,128)S(1)}, f32[2,2,8,512]{3,2,1,0:T(8,128)S(1)}, u32[]{:S(2)}, u32[]{:S(2)}) collective-permute-start(f32[2,2,8,512]{3,2,1,0:T(8,128)S(1)} %slice.31.refs_4_), channel_id=1, source_target_pairs={{0,8},{4,12},{8,0},{12,4},{1,9},{5,13},{9,1},{13,5},{2,10},{6,14},... | collective-permute-start | bytes 196616 | tf_op jit(solution)/shard_map/ppermute | solution.py:201
  7.1 5.4 %collective-permute-start.2 = (f32[2,2,8,512]{3,2,1,0:T(8,128)S(1)}, f32[2,2,8,512]{3,2,1,0:T(8,128)S(1)}, u32[]{:S(2)}, u32[]{:S(2)}) collective-permute-start(f32[2,2,8,512]{3,2,1,0:T(8,128)S(1)} %slice.31.refs_4_), channel_id=1, source_target_pairs={{0,4},{4,0},{8,12},{12,8},{1,5},{5,1},{9,13},{13,9},{2,6},{6,2},{1... | collective-permute-start | bytes 196616 | tf_op jit(solution)/shard_map/ppermute | solution.py:201
  7.2 0.7 %copy-start.1 = (s32[8]{0:T(128)S(1)}, s32[8]{0:T(128)}, u32[]{:S(2)}) copy-start(s32[8]{0:T(128)} %param.3) | copy-start | bytes 100
  8.1 7.8 %collective-permute-start.9 = (f32[2,2,4,512]{3,2,1,0:T(4,128)S(1)}, f32[2,2,4,512]{3,2,1,0:T(4,128)S(1)}, u32[]{:S(2)}, u32[]{:S(2)}) collective-permute-start(f32[2,2,4,512]{3,2,1,0:T(4,128)S(1)} %slice_select_fusion.2), channel_id=1, source_target_pairs={{6,1},{4,3},{5,2},{7,0},{2,5},{0,7},{1,6},{3,4},{14,9},{12,11},{13... | collective-permute-start | bytes 98312 | tf_op jit(solution)/shard_map/ppermute | solution.py:198
  9.2 4.5 %collective-permute-start.6 = (f32[2,2,8,512]{3,2,1,0:T(8,128)S(1)}, f32[2,2,8,512]{3,2,1,0:T(8,128)S(1)}, u32[]{:S(2)}, u32[]{:S(2)}) collective-permute-start(f32[2,2,8,512]{3,2,1,0:T(8,128)S(1)} %collective-permute-done.1.refs_3_), channel_id=1, source_target_pairs={{0,4},{4,0},{8,12},{12,8},{1,5},{5,1},{9,13},{13,9},{2,6},{6,2},{1... | collective-permute-start | bytes 196616 | tf_op jit(solution)/shard_map/ppermute | solution.py:201
  10.4 4.7 %collective-permute-start.5 = (f32[6,2,4,512]{3,2,1,0:T(4,128)S(1)}, f32[6,2,4,512]{3,2,1,0:T(4,128)S(1)}, u32[]{:S(2)}, u32[]{:S(2)}) collective-permute-start(f32[6,2,4,512]{3,2,1,0:T(4,128)S(1)} %get-tuple-element.15), channel_id=1, source_target_pairs={{1,2},{3,0},{2,1},{0,3},{5,6},{7,4},{6,5},{4,7},{9,10},{11,8},{10,... | collective-permute-start | bytes 294920 | tf_op jit(solution)/shard_map/ppermute | solution.py:193
  12.5 2.6 %collective-permute-start.4 = (f32[6,2,4,512]{3,2,1,0:T(4,128)S(1)}, f32[6,2,4,512]{3,2,1,0:T(4,128)S(1)}, u32[]{:S(2)}, u32[]{:S(2)}) collective-permute-start(f32[6,2,4,512]{3,2,1,0:T(4,128)S(1)} %get-tuple-element.16), channel_id=1, source_target_pairs={{0,1},{1,0},{2,3},{3,2},{4,5},{5,4},{6,7},{7,6},{8,9},{9,8},{10,11... | collective-permute-start | bytes 294920 | tf_op jit(solution)/shard_map/ppermute | solution.py:189
  12.5 4.5 %collective-permute-start.7 = (f32[2,2,8,512]{3,2,1,0:T(8,128)S(1)}, f32[2,2,8,512]{3,2,1,0:T(8,128)S(1)}, u32[]{:S(2)}, u32[]{:S(2)}) collective-permute-start(f32[2,2,8,512]{3,2,1,0:T(8,128)S(1)} %collective-permute-done.3.refs_6_), channel_id=1, source_target_pairs={{0,4},{4,0},{8,12},{12,8},{1,5},{5,1},{9,13},{13,9},{2,6},{6,2},{1... | collective-permute-start | bytes 196616 | tf_op jit(solution)/shard_map/ppermute | solution.py:201
  13.7 3.3 %collective-permute-start.8 = (f32[2,2,4,512]{3,2,1,0:T(4,128)S(1)}, f32[2,2,4,512]{3,2,1,0:T(4,128)S(1)}, u32[]{:S(2)}, u32[]{:S(2)}) collective-permute-start(f32[2,2,4,512]{3,2,1,0:T(4,128)S(1)} %slice_select_fusion.3), channel_id=1, source_target_pairs={{0,1},{1,0},{2,3},{3,2},{4,5},{5,4},{6,7},{7,6},{8,9},{9,8},{10,11... | collective-permute-start | bytes 98312 | tf_op jit(solution)/shard_map/ppermute | solution.py:189

commit v6 on v5

--- a/solution.py
+++ b/solution.py
@@ -237,12 +237,12 @@
         edge_2 = z(edge, 2)
         inner_2 = z(inner, 2)
         edge_1 = z(edge, 1)
-        inner_1 = z(inner, 1)
+        inner_1 = z(after(inner, edge), 1)
+        far_b = across(edge_2, 1)
         edge_3 = z(edge_2, 1)
         inner_3 = z(inner_2, 1)
         early = join(edge, edge_1, edge_2)
         far_a = rim_far(early)
-        far_b = across(edge_2, 1)
         near_a, near_b = rim_near(early), rim_near(after(edge_3, inner_1))
         slots = 3 * nd
         operands = [listed, edge, edge_1, edge_2, inner, inner_1, inner_2, near_a, far_a, band]

time: 18.4 us -> 18.2 us (0.989)
  waiting for transfers between devices: 2.56 us -> 2.18 us
    ppermute x6, waiting for transfers between devices: 2.26 us -> 1.88 us  [z(): return lax.ppermute(array, 'date', pairs_of(size, flip))]
  transfers between devices with their start and end apart: 10 -> 10, of which waited for: 5 -> 6; matrix products, arithmetic and copies ran while one was open for 1% -> 1% of each run, Pallas kernels for 5% -> 5%
where the time goes in v6:
time: 18.2 us; the launch traced here: 18 us
  starting transfers between devices  11.9 us (65%)
  waiting for transfers between devices  2.18 us (12%)
  Pallas kernels  2.15 us (12%)
  local copies, waits for them, and re-layouts  1.6 us (9%)
    ppermute x6, starting transfers between devices, z(): return lax.ppermute(array, 'date', pairs_of(size, flip))  8.5 us
    ppermute x6, waiting for transfers between devices, z(): return lax.ppermute(array, 'date', pairs_of(size, flip))  1.88 us
    pallas_call x1, Pallas kernels, body(): pl.pallas_call(functools.partial(kernel, ([nd], [nd], [nd]), nd, slots, '...  1.29 us
    ppermute x2, starting transfers between devices, rim_near(): return lax.ppermute(jnp.where(odd, first, last), 'row', near)  1.21 us
    ppermute x1, starting transfers between devices, rim_far(): return lax.ppermute(jnp.where(odd, last, first), 'row', far)  1.17 us
    ppermute x1, starting transfers between devices, across(): return lax.ppermute(jnp.where(odd, last, first), ('date', 'row'), pairs)  1.02 us
    slice x1, local copies, waits for them, and re-layouts, cut(): first, last = (block[:, :, :half], block[:, :, rows - half:])  0.93 us
    pallas_call x1, Pallas kernels, body(): pl.pallas_call(functools.partial(kernel, ([nd] * 3, [slots], [slots]), nd...  0.86 us
  transfers between devices with their start and end apart: 10, of which 6 were waited for; matrix products, arithmetic and copies ran while one was open for 1% of the time, Pallas kernels for 5%

profile of v6, /device:TPU:0, one launch (start us, length us, event | category | flops | bytes accessed | tf_op | source)
XLA Modules:
  0.0 18.0 jit_solution(16109424933420761491)
XLA Ops:
  0.0 0.0 copy-start
  0.0 0.9 %fusion.1 = (f32[2,2,4,512]{3,2,1,0:T(4,128)S(1)}, f32[2,2,4,512]{3,2,1,0:T(4,128)S(1)}) fusion(f32[2,2,16,512]{3,2,1,0:T(8,128)} %param.2), kind=kLoop, calls=%fused_computation.9 | loop fusion | bytes 131072 | tf_op jit(solution)/shard_map/slice | solution.py:184
  1.0 4.1 %collective-permute-start.1 = (f32[2,2,8,512]{3,2,1,0:T(8,128)S(1)}, f32[2,2,8,512]{3,2,1,0:T(8,128)S(1)}, u32[]{:S(2)}, u32[]{:S(2)}) collective-permute-start(f32[2,2,8,512]{3,2,1,0:T(8,128)S(1)} %pad_maximum_fusion.1.refs_1_), channel_id=1, source_target_pairs={{0,8},{4,12},{8,0},{12,4},{1,9},{5,13},{9,1},{13,5},{2,10},{6,14},... | collective-permute-start | bytes 196616 | tf_op jit(solution)/shard_map/ppermute | solution.py:201
  5.1 1.6 %collective-permute-start = (f32[2,2,8,512]{3,2,1,0:T(8,128)S(1)}, f32[2,2,8,512]{3,2,1,0:T(8,128)S(1)}, u32[]{:S(2)}, u32[]{:S(2)}) collective-permute-start(f32[2,2,8,512]{3,2,1,0:T(8,128)S(1)} %pad_maximum_fusion.1.refs_1_), channel_id=1, source_target_pairs={{0,4},{4,0},{8,12},{12,8},{1,5},{5,1},{9,13},{13,9},{2,6},{6,2},{1... | collective-permute-start | bytes 196616 | tf_op jit(solution)/shard_map/ppermute | solution.py:201
  6.6 0.0 copy-done
  6.7 0.4 %collective-permute-start.3 = (f32[2,2,8,512]{3,2,1,0:T(8,128)S(1)}, f32[2,2,8,512]{3,2,1,0:T(8,128)S(1)}, u32[]{:S(2)}, u32[]{:S(2)}) collective-permute-start(f32[2,2,8,512]{3,2,1,0:T(8,128)S(1)} %slice.31.refs_4_), channel_id=1, source_target_pairs={{0,8},{4,12},{8,0},{12,4},{1,9},{5,13},{9,1},{13,5},{2,10},{6,14},... | collective-permute-start | bytes 196616 | tf_op jit(solution)/shard_map/ppermute | solution.py:201
  7.1 0.2 %collective-permute-start.2 = (f32[2,2,8,512]{3,2,1,0:T(8,128)S(1)}, f32[2,2,8,512]{3,2,1,0:T(8,128)S(1)}, u32[]{:S(2)}, u32[]{:S(2)}) collective-permute-start(f32[2,2,8,512]{3,2,1,0:T(8,128)S(1)} %slice.31.refs_4_), channel_id=1, source_target_pairs={{0,4},{4,0},{8,12},{12,8},{1,5},{5,1},{9,13},{13,9},{2,6},{6,2},{1... | collective-permute-start | bytes 196616 | tf_op jit(solution)/shard_map/ppermute | solution.py:201
  7.2 0.0 copy-start.1
  7.3 0.7 %copy-done.1 = s32[8]{0:T(128)S(1)} copy-done((s32[8]{0:T(128)S(1)}, s32[8]{0:T(128)}, u32[]{:S(2)}) %copy-start.1) | copy-done | bytes 56
  8.0 0.2 collective-permute-done.1.refs_3_
  8.1 1.0 %collective-permute-start.9 = (f32[2,2,4,512]{3,2,1,0:T(4,128)S(1)}, f32[2,2,4,512]{3,2,1,0:T(4,128)S(1)}, u32[]{:S(2)}, u32[]{:S(2)}) collective-permute-start(f32[2,2,4,512]{3,2,1,0:T(4,128)S(1)} %slice_select_fusion.2), channel_id=1, source_target_pairs={{6,1},{4,3},{5,2},{7,0},{2,5},{0,7},{1,6},{3,4},{14,9},{12,11},{13... | collective-permute-start | bytes 98312 | tf_op jit(solution)/shard_map/ppermute | solution.py:198
  9.2 1.2 %collective-permute-start.6 = (f32[2,2,8,512]{3,2,1,0:T(8,128)S(1)}, f32[2,2,8,512]{3,2,1,0:T(8,128)S(1)}, u32[]{:S(2)}, u32[]{:S(2)}) collective-permute-start(f32[2,2,8,512]{3,2,1,0:T(8,128)S(1)} %collective-permute-done.1.refs_3_), channel_id=1, source_target_pairs={{0,4},{4,0},{8,12},{12,8},{1,5},{5,1},{9,13},{13,9},{2,6},{6,2},{1... | collective-permute-start | bytes 196616 | tf_op jit(solution)/shard_map/ppermute | solution.py:201
  10.3 0.0 collective-permute-done.refs_2_
  10.4 1.2 %collective-permute-start.5 = (f32[6,2,4,512]{3,2,1,0:T(4,128)S(1)}, f32[6,2,4,512]{3,2,1,0:T(4,128)S(1)}, u32[]{:S(2)}, u32[]{:S(2)}) collective-permute-start(f32[6,2,4,512]{3,2,1,0:T(4,128)S(1)} %get-tuple-element.17), channel_id=1, source_target_pairs={{1,2},{3,0},{2,1},{0,3},{5,6},{7,4},{6,5},{4,7},{9,10},{11,8},{10,... | collective-permute-start | bytes 294920 | tf_op jit(solution)/shard_map/ppermute | solution.py:193
  11.6 0.4 %collective-permute-done.2.refs_5_ = f32[2,2,8,512]{3,2,1,0:T(8,128)S(1)} collective-permute-done((f32[2,2,8,512]{3,2,1,0:T(8,128)S(1)}, f32[2,2,8,512]{3,2,1,0:T(8,128)S(1)}, u32[]{:S(2)}, u32[]{:S(2)}) %collective-permute-start.2) | collective-permute-done | bytes 65568 | tf_op jit(solution)/shard_map/ppermute | solution.py:201
  12.0 0.1 collective-permute-start.4
  12.1 0.4 %collective-permute-done.3.refs_6_ = f32[2,2,8,512]{3,2,1,0:T(8,128)S(1)} collective-permute-done((f32[2,2,8,512]{3,2,1,0:T(8,128)S(1)}, f32[2,2,8,512]{3,2,1,0:T(8,128)S(1)}, u32[]{:S(2)}, u32[]{:S(2)}) %collective-permute-start.3) | collective-permute-done | bytes 65568 | tf_op jit(solution)/shard_map/ppermute | solution.py:201
  12.5 1.1 %collective-permute-start.7 = (f32[2,2,8,512]{3,2,1,0:T(8,128)S(1)}, f32[2,2,8,512]{3,2,1,0:T(8,128)S(1)}, u32[]{:S(2)}, u32[]{:S(2)}) collective-permute-start(f32[2,2,8,512]{3,2,1,0:T(8,128)S(1)} %collective-permute-done.3.refs_6_), channel_id=1, source_target_pairs={{0,4},{4,0},{8,12},{12,8},{1,5},{5,1},{9,13},{13,9},{2,6},{6,2},{1... | collective-permute-start | bytes 196616 | tf_op jit(solution)/shard_map/ppermute | solution.py:201
  13.5 0.1 collective-permute-done.6.refs_4_
  13.7 1.1 %collective-permute-start.8 = (f32[2,2,4,512]{3,2,1,0:T(4,128)S(1)}, f32[2,2,4,512]{3,2,1,0:T(4,128)S(1)}, u32[]{:S(2)}, u32[]{:S(2)}) collective-permute-start(f32[2,2,4,512]{3,2,1,0:T(4,128)S(1)} %slice_select_fusion.3), channel_id=1, source_target_pairs={{0,1},{1,0},{2,3},{3,2},{4,5},{5,4},{6,7},{7,6},{8,9},{9,8},{10,11... | collective-permute-start | bytes 98312 | tf_op jit(solution)/shard_map/ppermute | solution.py:189
  14.8 0.3 %collective-permute-done.5.refs_8_ = f32[6,2,4,512]{3,2,1,0:T(4,128)S(1)} collective-permute-done((f32[6,2,4,512]{3,2,1,0:T(4,128)S(1)}, f32[6,2,4,512]{3,2,1,0:T(4,128)S(1)}, u32[]{:S(2)}, u32[]{:S(2)}) %collective-permute-start.5) | collective-permute-done | bytes 98336 | tf_op jit(solution)/shard_map/ppermute | solution.py:193
  15.1 0.0 collective-permute-done.4.refs_7_
  15.1 0.9 %early_dates.1 = (f32[2,2,24,512]{3,2,1,0:T(8,128)S(1)}, f32[2,16,512]{2,1,0:T(8,128)S(1)}, f32[2,6,2,16,512]{4,3,2,1,0:T(8,128)S(1)}, s32[1,128]{1,0:T(1,128)S(1)}) custom-call(s32[1,8]{1,0:T(1,128)S(1)} %maximum_bitcast_fusion.refs_0_, f32[2,2,8,512]{3,2,1,0:T(8,128)S(1)} %pad_maximum_fusion.1.refs_1_, f32[2,2,8,512]{3,2,1,0:T(8,128)S(1)} %collective-permute-done.refs_2_, ...), custom_call_target="tpu_custom_call" | custom-call | flops 805306368 | bytes 1572864 | tf_op jit(solution)/shard_map/early_dates/pallas_call | solution.py:249
  15.9 0.0 collective-permute-done.9.refs_7_
  16.0 0.8 %collective-permute-done.7.refs_5_ = f32[2,2,8,512]{3,2,1,0:T(8,128)S(1)} collective-permute-done((f32[2,2,8,512]{3,2,1,0:T(8,128)S(1)}, f32[2,2,8,512]{3,2,1,0:T(8,128)S(1)}, u32[]{:S(2)}, u32[]{:S(2)}) %collective-permute-start.7) | collective-permute-done | bytes 65568 | tf_op jit(solution)/shard_map/ppermute | solution.py:201
  16.8 0.0 collective-permute-done.8.refs_6_
  16.8 1.3 %last_dates.1 = f32[2,8,2,16,512]{4,3,2,1,0:T(8,128)} custom-call(s32[1,128]{1,0:T(1,128)S(1)} %get-tuple-element.12.refs_0_, f32[2,2,24,512]{3,2,1,0:T(8,128)S(1)} %get-tuple-element.13.refs_1_, f32[2,16,512]{2,1,0:T(8,128)S(1)} %get-tuple-element.14.refs_2_, f32[2,6,2,16,512]{4,3,2,1,0:T(8,128)S(1)} %get-tuple-element.15.refs_3_, ...), custom_call_target="tpu_custom_call" | custom-call | flops 268435456 | bytes 524288 | tf_op jit(solution)/shard_map/last_dates/pallas_call | solution.py:265
  (8 shorter events, 0.2 us)
Async XLA Ops:
  0.0 6.6 %copy-start = (f32[2,2,16,512]{3,2,1,0:T(8,128)S(1)}, f32[2,2,16,512]{3,2,1,0:T(8,128)}, u32[]{:S(2)}) copy-start(f32[2,2,16,512]{3,2,1,0:T(8,128)} %param.2) | copy-start | bytes 393220
  1.0 7.2 %collective-permute-start.1 = (f32[2,2,8,512]{3,2,1,0:T(8,128)S(1)}, f32[2,2,8,512]{3,2,1,0:T(8,128)S(1)}, u32[]{:S(2)}, u32[]{:S(2)}) collective-permute-start(f32[2,2,8,512]{3,2,1,0:T(8,128)S(1)} %pad_maximum_fusion.1.refs_1_), channel_id=1, source_target_pairs={{0,8},{4,12},{8,0},{12,4},{1,9},{5,13},{9,1},{13,5},{2,10},{6,14},... | collective-permute-start | bytes 196616 | tf_op jit(solution)/shard_map/ppermute | solution.py:201
  5.1 5.3 %collective-permute-start = (f32[2,2,8,512]{3,2,1,0:T(8,128)S(1)}, f32[2,2,8,512]{3,2,1,0:T(8,128)S(1)}, u32[]{:S(2)}, u32[]{:S(2)}) collective-permute-start(f32[2,2,8,512]{3,2,1,0:T(8,128)S(1)} %pad_maximum_fusion.1.refs_1_), channel_id=1, source_target_pairs={{0,4},{4,0},{8,12},{12,8},{1,5},{5,1},{9,13},{13,9},{2,6},{6,2},{1... | collective-permute-start | bytes 196616 | tf_op jit(solution)/shard_map/ppermute | solution.py:201
  6.7 5.8 %collective-permute-start.3 = (f32[2,2,8,512]{3,2,1,0:T(8,128)S(1)}, f32[2,2,8,512]{3,2,1,0:T(8,128)S(1)}, u32[]{:S(2)}, u32[]{:S(2)}) collective-permute-start(f32[2,2,8,512]{3,2,1,0:T(8,128)S(1)} %slice.31.refs_4_), channel_id=1, source_target_pairs={{0,8},{4,12},{8,0},{12,4},{1,9},{5,13},{9,1},{13,5},{2,10},{6,14},... | collective-permute-start | bytes 196616 | tf_op jit(solution)/shard_map/ppermute | solution.py:201
  7.1 4.9 %collective-permute-start.2 = (f32[2,2,8,512]{3,2,1,0:T(8,128)S(1)}, f32[2,2,8,512]{3,2,1,0:T(8,128)S(1)}, u32[]{:S(2)}, u32[]{:S(2)}) collective-permute-start(f32[2,2,8,512]{3,2,1,0:T(8,128)S(1)} %slice.31.refs_4_), channel_id=1, source_target_pairs={{0,4},{4,0},{8,12},{12,8},{1,5},{5,1},{9,13},{13,9},{2,6},{6,2},{1... | collective-permute-start | bytes 196616 | tf_op jit(solution)/shard_map/ppermute | solution.py:201
  7.2 0.7 %copy-start.1 = (s32[8]{0:T(128)S(1)}, s32[8]{0:T(128)}, u32[]{:S(2)}) copy-start(s32[8]{0:T(128)} %param.3) | copy-start | bytes 100
  8.1 7.8 %collective-permute-start.9 = (f32[2,2,4,512]{3,2,1,0:T(4,128)S(1)}, f32[2,2,4,512]{3,2,1,0:T(4,128)S(1)}, u32[]{:S(2)}, u32[]{:S(2)}) collective-permute-start(f32[2,2,4,512]{3,2,1,0:T(4,128)S(1)} %slice_select_fusion.2), channel_id=1, source_target_pairs={{6,1},{4,3},{5,2},{7,0},{2,5},{0,7},{1,6},{3,4},{14,9},{12,11},{13... | collective-permute-start | bytes 98312 | tf_op jit(solution)/shard_map/ppermute | solution.py:198
  9.2 4.5 %collective-permute-start.6 = (f32[2,2,8,512]{3,2,1,0:T(8,128)S(1)}, f32[2,2,8,512]{3,2,1,0:T(8,128)S(1)}, u32[]{:S(2)}, u32[]{:S(2)}) collective-permute-start(f32[2,2,8,512]{3,2,1,0:T(8,128)S(1)} %collective-permute-done.1.refs_3_), channel_id=1, source_target_pairs={{0,4},{4,0},{8,12},{12,8},{1,5},{5,1},{9,13},{13,9},{2,6},{6,2},{1... | collective-permute-start | bytes 196616 | tf_op jit(solution)/shard_map/ppermute | solution.py:201
  10.4 4.7 %collective-permute-start.5 = (f32[6,2,4,512]{3,2,1,0:T(4,128)S(1)}, f32[6,2,4,512]{3,2,1,0:T(4,128)S(1)}, u32[]{:S(2)}, u32[]{:S(2)}) collective-permute-start(f32[6,2,4,512]{3,2,1,0:T(4,128)S(1)} %get-tuple-element.17), channel_id=1, source_target_pairs={{1,2},{3,0},{2,1},{0,3},{5,6},{7,4},{6,5},{4,7},{9,10},{11,8},{10,... | collective-permute-start | bytes 294920 | tf_op jit(solution)/shard_map/ppermute | solution.py:193
  12.0 3.1 %collective-permute-start.4 = (f32[6,2,4,512]{3,2,1,0:T(4,128)S(1)}, f32[6,2,4,512]{3,2,1,0:T(4,128)S(1)}, u32[]{:S(2)}, u32[]{:S(2)}) collective-permute-start(f32[6,2,4,512]{3,2,1,0:T(4,128)S(1)} %get-tuple-element.18), channel_id=1, source_target_pairs={{0,1},{1,0},{2,3},{3,2},{4,5},{5,4},{6,7},{7,6},{8,9},{9,8},{10,11... | collective-permute-start | bytes 294920 | tf_op jit(solution)/shard_map/ppermute | solution.py:189
  12.5 4.3 %collective-permute-start.7 = (f32[2,2,8,512]{3,2,1,0:T(8,128)S(1)}, f32[2,2,8,512]{3,2,1,0:T(8,128)S(1)}, u32[]{:S(2)}, u32[]{:S(2)}) collective-permute-start(f32[2,2,8,512]{3,2,1,0:T(8,128)S(1)} %collective-permute-done.3.refs_6_), channel_id=1, source_target_pairs={{0,4},{4,0},{8,12},{12,8},{1,5},{5,1},{9,13},{13,9},{2,6},{6,2},{1... | collective-permute-start | bytes 196616 | tf_op jit(solution)/shard_map/ppermute | solution.py:201
  13.7 3.1 %collective-permute-start.8 = (f32[2,2,4,512]{3,2,1,0:T(4,128)S(1)}, f32[2,2,4,512]{3,2,1,0:T(4,128)S(1)}, u32[]{:S(2)}, u32[]{:S(2)}) collective-permute-start(f32[2,2,4,512]{3,2,1,0:T(4,128)S(1)} %slice_select_fusion.3), channel_id=1, source_target_pairs={{0,1},{1,0},{2,3},{3,2},{4,5},{5,4},{6,7},{7,6},{8,9},{9,8},{10,11... | collective-permute-start | bytes 98312 | tf_op jit(solution)/shard_map/ppermute | solution.py:189

commit v7 on v6

--- a/solution.py
+++ b/solution.py
@@ -149,13 +149,13 @@
         fields = [power_of(re, im)]
         for d in range(nd):
             fields += cross_of(own_ref[d, 0], own_ref[d, 1], re, im)
-        res[s] = columns(fields)
-        power = res[s, :rows]
+        sums = columns(fields)
+        power = sums[:rows]
         for d in range(nd):
             factor = scale(own_power[d], power)
             at = (1 + 2 * d) * rows
-            buf[d, s, 0] = res[s, at:at + rows] * factor
-            buf[d, s, 1] = res[s, at + rows:at + 2 * rows] * factor
+            buf[d, s, 0] = sums[at:at + rows] * factor
+            buf[d, s, 1] = sums[at + rows:at + 2 * rows] * factor
         if stage == "last" and s == 0:
             for t in range(own):
                 send(done.at[:, t], t)

time: 18.2 us -> 18.2 us (level)
  no operation moved by 1% of the time
where the time goes in v7:
time: 18.2 us; the launch traced here: 18 us
  starting transfers between devices  11.9 us (65%)
  waiting for transfers between devices  2.18 us (12%)
  Pallas kernels  2.15 us (12%)
  local copies, waits for them, and re-layouts  1.6 us (9%)
    ppermute x6, starting transfers between devices, z(): return lax.ppermute(array, 'date', pairs_of(size, flip))  8.5 us
    ppermute x6, waiting for transfers between devices, z(): return lax.ppermute(array, 'date', pairs_of(size, flip))  1.88 us
    pallas_call x1, Pallas kernels, body(): pl.pallas_call(functools.partial(kernel, ([nd], [nd], [nd]), nd, slots, '...  1.29 us
    ppermute x2, starting transfers between devices, rim_near(): return lax.ppermute(jnp.where(odd, first, last), 'row', near)  1.21 us
    ppermute x1, starting transfers between devices, rim_far(): return lax.ppermute(jnp.where(odd, last, first), 'row', far)  1.17 us
    ppermute x1, starting transfers between devices, across(): return lax.ppermute(jnp.where(odd, last, first), ('date', 'row'), pairs)  1.02 us
    slice x1, local copies, waits for them, and re-layouts, cut(): first, last = (block[:, :, :half], block[:, :, rows - half:])  0.93 us
    pallas_call x1, Pallas kernels, body(): pl.pallas_call(functools.partial(kernel, ([nd] * 3, [slots], [slots]), nd...  0.86 us
  transfers between devices with their start and end apart: 10, of which 6 were waited for; matrix products, arithmetic and copies ran while one was open for 1% of the time, Pallas kernels for 5%

profile of v7, /device:TPU:0, one launch (start us, length us, event | category | flops | bytes accessed | tf_op | source)
XLA Modules:
  0.0 18.0 jit_solution(16109424933420761491)
XLA Ops:
  0.0 0.0 copy-start
  0.0 0.9 %fusion.1 = (f32[2,2,4,512]{3,2,1,0:T(4,128)S(1)}, f32[2,2,4,512]{3,2,1,0:T(4,128)S(1)}) fusion(f32[2,2,16,512]{3,2,1,0:T(8,128)} %param.2), kind=kLoop, calls=%fused_computation.9 | loop fusion | bytes 131072 | tf_op jit(solution)/shard_map/slice | solution.py:184
  1.0 4.1 %collective-permute-start.1 = (f32[2,2,8,512]{3,2,1,0:T(8,128)S(1)}, f32[2,2,8,512]{3,2,1,0:T(8,128)S(1)}, u32[]{:S(2)}, u32[]{:S(2)}) collective-permute-start(f32[2,2,8,512]{3,2,1,0:T(8,128)S(1)} %pad_maximum_fusion.1.refs_1_), channel_id=1, source_target_pairs={{0,8},{4,12},{8,0},{12,4},{1,9},{5,13},{9,1},{13,5},{2,10},{6,14},... | collective-permute-start | bytes 196616 | tf_op jit(solution)/shard_map/ppermute | solution.py:201
  5.1 1.6 %collective-permute-start = (f32[2,2,8,512]{3,2,1,0:T(8,128)S(1)}, f32[2,2,8,512]{3,2,1,0:T(8,128)S(1)}, u32[]{:S(2)}, u32[]{:S(2)}) collective-permute-start(f32[2,2,8,512]{3,2,1,0:T(8,128)S(1)} %pad_maximum_fusion.1.refs_1_), channel_id=1, source_target_pairs={{0,4},{4,0},{8,12},{12,8},{1,5},{5,1},{9,13},{13,9},{2,6},{6,2},{1... | collective-permute-start | bytes 196616 | tf_op jit(solution)/shard_map/ppermute | solution.py:201
  6.6 0.0 copy-done
  6.7 0.4 %collective-permute-start.3 = (f32[2,2,8,512]{3,2,1,0:T(8,128)S(1)}, f32[2,2,8,512]{3,2,1,0:T(8,128)S(1)}, u32[]{:S(2)}, u32[]{:S(2)}) collective-permute-start(f32[2,2,8,512]{3,2,1,0:T(8,128)S(1)} %slice.31.refs_4_), channel_id=1, source_target_pairs={{0,8},{4,12},{8,0},{12,4},{1,9},{5,13},{9,1},{13,5},{2,10},{6,14},... | collective-permute-start | bytes 196616 | tf_op jit(solution)/shard_map/ppermute | solution.py:201
  7.1 0.2 %collective-permute-start.2 = (f32[2,2,8,512]{3,2,1,0:T(8,128)S(1)}, f32[2,2,8,512]{3,2,1,0:T(8,128)S(1)}, u32[]{:S(2)}, u32[]{:S(2)}) collective-permute-start(f32[2,2,8,512]{3,2,1,0:T(8,128)S(1)} %slice.31.refs_4_), channel_id=1, source_target_pairs={{0,4},{4,0},{8,12},{12,8},{1,5},{5,1},{9,13},{13,9},{2,6},{6,2},{1... | collective-permute-start | bytes 196616 | tf_op jit(solution)/shard_map/ppermute | solution.py:201
  7.2 0.0 copy-start.1
  7.3 0.7 %copy-done.1 = s32[8]{0:T(128)S(1)} copy-done((s32[8]{0:T(128)S(1)}, s32[8]{0:T(128)}, u32[]{:S(2)}) %copy-start.1) | copy-done | bytes 56
  8.0 0.2 collective-permute-done.1.refs_3_
  8.1 1.0 %collective-permute-start.9 = (f32[2,2,4,512]{3,2,1,0:T(4,128)S(1)}, f32[2,2,4,512]{3,2,1,0:T(4,128)S(1)}, u32[]{:S(2)}, u32[]{:S(2)}) collective-permute-start(f32[2,2,4,512]{3,2,1,0:T(4,128)S(1)} %slice_select_fusion.2), channel_id=1, source_target_pairs={{6,1},{4,3},{5,2},{7,0},{2,5},{0,7},{1,6},{3,4},{14,9},{12,11},{13... | collective-permute-start | bytes 98312 | tf_op jit(solution)/shard_map/ppermute | solution.py:198
  9.2 1.2 %collective-permute-start.6 = (f32[2,2,8,512]{3,2,1,0:T(8,128)S(1)}, f32[2,2,8,512]{3,2,1,0:T(8,128)S(1)}, u32[]{:S(2)}, u32[]{:S(2)}) collective-permute-start(f32[2,2,8,512]{3,2,1,0:T(8,128)S(1)} %collective-permute-done.1.refs_3_), channel_id=1, source_target_pairs={{0,4},{4,0},{8,12},{12,8},{1,5},{5,1},{9,13},{13,9},{2,6},{6,2},{1... | collective-permute-start | bytes 196616 | tf_op jit(solution)/shard_map/ppermute | solution.py:201
  10.3 0.0 collective-permute-done.refs_2_
  10.4 1.2 %collective-permute-start.5 = (f32[6,2,4,512]{3,2,1,0:T(4,128)S(1)}, f32[6,2,4,512]{3,2,1,0:T(4,128)S(1)}, u32[]{:S(2)}, u32[]{:S(2)}) collective-permute-start(f32[6,2,4,512]{3,2,1,0:T(4,128)S(1)} %get-tuple-element.17), channel_id=1, source_target_pairs={{1,2},{3,0},{2,1},{0,3},{5,6},{7,4},{6,5},{4,7},{9,10},{11,8},{10,... | collective-permute-start | bytes 294920 | tf_op jit(solution)/shard_map/ppermute | solution.py:193
  11.6 0.4 %collective-permute-done.2.refs_5_ = f32[2,2,8,512]{3,2,1,0:T(8,128)S(1)} collective-permute-done((f32[2,2,8,512]{3,2,1,0:T(8,128)S(1)}, f32[2,2,8,512]{3,2,1,0:T(8,128)S(1)}, u32[]{:S(2)}, u32[]{:S(2)}) %collective-permute-start.2) | collective-permute-done | bytes 65568 | tf_op jit(solution)/shard_map/ppermute | solution.py:201
  12.0 0.1 collective-permute-start.4
  12.1 0.4 %collective-permute-done.3.refs_6_ = f32[2,2,8,512]{3,2,1,0:T(8,128)S(1)} collective-permute-done((f32[2,2,8,512]{3,2,1,0:T(8,128)S(1)}, f32[2,2,8,512]{3,2,1,0:T(8,128)S(1)}, u32[]{:S(2)}, u32[]{:S(2)}) %collective-permute-start.3) | collective-permute-done | bytes 65568 | tf_op jit(solution)/shard_map/ppermute | solution.py:201
  12.5 1.1 %collective-permute-start.7 = (f32[2,2,8,512]{3,2,1,0:T(8,128)S(1)}, f32[2,2,8,512]{3,2,1,0:T(8,128)S(1)}, u32[]{:S(2)}, u32[]{:S(2)}) collective-permute-start(f32[2,2,8,512]{3,2,1,0:T(8,128)S(1)} %collective-permute-done.3.refs_6_), channel_id=1, source_target_pairs={{0,4},{4,0},{8,12},{12,8},{1,5},{5,1},{9,13},{13,9},{2,6},{6,2},{1... | collective-permute-start | bytes 196616 | tf_op jit(solution)/shard_map/ppermute | solution.py:201
  13.5 0.1 collective-permute-done.6.refs_4_
  13.7 1.1 %collective-permute-start.8 = (f32[2,2,4,512]{3,2,1,0:T(4,128)S(1)}, f32[2,2,4,512]{3,2,1,0:T(4,128)S(1)}, u32[]{:S(2)}, u32[]{:S(2)}) collective-permute-start(f32[2,2,4,512]{3,2,1,0:T(4,128)S(1)} %slice_select_fusion.3), channel_id=1, source_target_pairs={{0,1},{1,0},{2,3},{3,2},{4,5},{5,4},{6,7},{7,6},{8,9},{9,8},{10,11... | collective-permute-start | bytes 98312 | tf_op jit(solution)/shard_map/ppermute | solution.py:189
  14.8 0.3 %collective-permute-done.5.refs_8_ = f32[6,2,4,512]{3,2,1,0:T(4,128)S(1)} collective-permute-done((f32[6,2,4,512]{3,2,1,0:T(4,128)S(1)}, f32[6,2,4,512]{3,2,1,0:T(4,128)S(1)}, u32[]{:S(2)}, u32[]{:S(2)}) %collective-permute-start.5) | collective-permute-done | bytes 98336 | tf_op jit(solution)/shard_map/ppermute | solution.py:193
  15.1 0.0 collective-permute-done.4.refs_7_
  15.1 0.9 %early_dates.1 = (f32[2,2,24,512]{3,2,1,0:T(8,128)S(1)}, f32[2,16,512]{2,1,0:T(8,128)S(1)}, f32[2,6,2,16,512]{4,3,2,1,0:T(8,128)S(1)}, s32[1,128]{1,0:T(1,128)S(1)}) custom-call(s32[1,8]{1,0:T(1,128)S(1)} %maximum_bitcast_fusion.refs_0_, f32[2,2,8,512]{3,2,1,0:T(8,128)S(1)} %pad_maximum_fusion.1.refs_1_, f32[2,2,8,512]{3,2,1,0:T(8,128)S(1)} %collective-permute-done.refs_2_, ...), custom_call_target="tpu_custom_call" | custom-call | flops 805306368 | bytes 1572864 | tf_op jit(solution)/shard_map/early_dates/pallas_call | solution.py:249
  15.9 0.0 collective-permute-done.9.refs_7_
  16.0 0.8 %collective-permute-done.7.refs_5_ = f32[2,2,8,512]{3,2,1,0:T(8,128)S(1)} collective-permute-done((f32[2,2,8,512]{3,2,1,0:T(8,128)S(1)}, f32[2,2,8,512]{3,2,1,0:T(8,128)S(1)}, u32[]{:S(2)}, u32[]{:S(2)}) %collective-permute-start.7) | collective-permute-done | bytes 65568 | tf_op jit(solution)/shard_map/ppermute | solution.py:201
  16.8 0.0 collective-permute-done.8.refs_6_
  16.8 1.3 %last_dates.1 = f32[2,8,2,16,512]{4,3,2,1,0:T(8,128)} custom-call(s32[1,128]{1,0:T(1,128)S(1)} %get-tuple-element.12.refs_0_, f32[2,2,24,512]{3,2,1,0:T(8,128)S(1)} %get-tuple-element.13.refs_1_, f32[2,16,512]{2,1,0:T(8,128)S(1)} %get-tuple-element.14.refs_2_, f32[2,6,2,16,512]{4,3,2,1,0:T(8,128)S(1)} %get-tuple-element.15.refs_3_, ...), custom_call_target="tpu_custom_call" | custom-call | flops 268435456 | bytes 524288 | tf_op jit(solution)/shard_map/last_dates/pallas_call | solution.py:265
  (8 shorter events, 0.2 us)
Async XLA Ops:
  0.0 6.6 %copy-start = (f32[2,2,16,512]{3,2,1,0:T(8,128)S(1)}, f32[2,2,16,512]{3,2,1,0:T(8,128)}, u32[]{:S(2)}) copy-start(f32[2,2,16,512]{3,2,1,0:T(8,128)} %param.2) | copy-start | bytes 393220
  1.0 7.2 %collective-permute-start.1 = (f32[2,2,8,512]{3,2,1,0:T(8,128)S(1)}, f32[2,2,8,512]{3,2,1,0:T(8,128)S(1)}, u32[]{:S(2)}, u32[]{:S(2)}) collective-permute-start(f32[2,2,8,512]{3,2,1,0:T(8,128)S(1)} %pad_maximum_fusion.1.refs_1_), channel_id=1, source_target_pairs={{0,8},{4,12},{8,0},{12,4},{1,9},{5,13},{9,1},{13,5},{2,10},{6,14},... | collective-permute-start | bytes 196616 | tf_op jit(solution)/shard_map/ppermute | solution.py:201
  5.1 5.3 %collective-permute-start = (f32[2,2,8,512]{3,2,1,0:T(8,128)S(1)}, f32[2,2,8,512]{3,2,1,0:T(8,128)S(1)}, u32[]{:S(2)}, u32[]{:S(2)}) collective-permute-start(f32[2,2,8,512]{3,2,1,0:T(8,128)S(1)} %pad_maximum_fusion.1.refs_1_), channel_id=1, source_target_pairs={{0,4},{4,0},{8,12},{12,8},{1,5},{5,1},{9,13},{13,9},{2,6},{6,2},{1... | collective-permute-start | bytes 196616 | tf_op jit(solution)/shard_map/ppermute | solution.py:201
  6.7 5.8 %collective-permute-start.3 = (f32[2,2,8,512]{3,2,1,0:T(8,128)S(1)}, f32[2,2,8,512]{3,2,1,0:T(8,128)S(1)}, u32[]{:S(2)}, u32[]{:S(2)}) collective-permute-start(f32[2,2,8,512]{3,2,1,0:T(8,128)S(1)} %slice.31.refs_4_), channel_id=1, source_target_pairs={{0,8},{4,12},{8,0},{12,4},{1,9},{5,13},{9,1},{13,5},{2,10},{6,14},... | collective-permute-start | bytes 196616 | tf_op jit(solution)/shard_map/ppermute | solution.py:201
  7.1 4.9 %collective-permute-start.2 = (f32[2,2,8,512]{3,2,1,0:T(8,128)S(1)}, f32[2,2,8,512]{3,2,1,0:T(8,128)S(1)}, u32[]{:S(2)}, u32[]{:S(2)}) collective-permute-start(f32[2,2,8,512]{3,2,1,0:T(8,128)S(1)} %slice.31.refs_4_), channel_id=1, source_target_pairs={{0,4},{4,0},{8,12},{12,8},{1,5},{5,1},{9,13},{13,9},{2,6},{6,2},{1... | collective-permute-start | bytes 196616 | tf_op jit(solution)/shard_map/ppermute | solution.py:201
  7.2 0.7 %copy-start.1 = (s32[8]{0:T(128)S(1)}, s32[8]{0:T(128)}, u32[]{:S(2)}) copy-start(s32[8]{0:T(128)} %param.3) | copy-start | bytes 100
  8.1 7.8 %collective-permute-start.9 = (f32[2,2,4,512]{3,2,1,0:T(4,128)S(1)}, f32[2,2,4,512]{3,2,1,0:T(4,128)S(1)}, u32[]{:S(2)}, u32[]{:S(2)}) collective-permute-start(f32[2,2,4,512]{3,2,1,0:T(4,128)S(1)} %slice_select_fusion.2), channel_id=1, source_target_pairs={{6,1},{4,3},{5,2},{7,0},{2,5},{0,7},{1,6},{3,4},{14,9},{12,11},{13... | collective-permute-start | bytes 98312 | tf_op jit(solution)/shard_map/ppermute | solution.py:198
  9.2 4.5 %collective-permute-start.6 = (f32[2,2,8,512]{3,2,1,0:T(8,128)S(1)}, f32[2,2,8,512]{3,2,1,0:T(8,128)S(1)}, u32[]{:S(2)}, u32[]{:S(2)}) collective-permute-start(f32[2,2,8,512]{3,2,1,0:T(8,128)S(1)} %collective-permute-done.1.refs_3_), channel_id=1, source_target_pairs={{0,4},{4,0},{8,12},{12,8},{1,5},{5,1},{9,13},{13,9},{2,6},{6,2},{1... | collective-permute-start | bytes 196616 | tf_op jit(solution)/shard_map/ppermute | solution.py:201
  10.4 4.7 %collective-permute-start.5 = (f32[6,2,4,512]{3,2,1,0:T(4,128)S(1)}, f32[6,2,4,512]{3,2,1,0:T(4,128)S(1)}, u32[]{:S(2)}, u32[]{:S(2)}) collective-permute-start(f32[6,2,4,512]{3,2,1,0:T(4,128)S(1)} %get-tuple-element.17), channel_id=1, source_target_pairs={{1,2},{3,0},{2,1},{0,3},{5,6},{7,4},{6,5},{4,7},{9,10},{11,8},{10,... | collective-permute-start | bytes 294920 | tf_op jit(solution)/shard_map/ppermute | solution.py:193
  12.0 3.1 %collective-permute-start.4 = (f32[6,2,4,512]{3,2,1,0:T(4,128)S(1)}, f32[6,2,4,512]{3,2,1,0:T(4,128)S(1)}, u32[]{:S(2)}, u32[]{:S(2)}) collective-permute-start(f32[6,2,4,512]{3,2,1,0:T(4,128)S(1)} %get-tuple-element.18), channel_id=1, source_target_pairs={{0,1},{1,0},{2,3},{3,2},{4,5},{5,4},{6,7},{7,6},{8,9},{9,8},{10,11... | collective-permute-start | bytes 294920 | tf_op jit(solution)/shard_map/ppermute | solution.py:189
  12.5 4.3 %collective-permute-start.7 = (f32[2,2,8,512]{3,2,1,0:T(8,128)S(1)}, f32[2,2,8,512]{3,2,1,0:T(8,128)S(1)}, u32[]{:S(2)}, u32[]{:S(2)}) collective-permute-start(f32[2,2,8,512]{3,2,1,0:T(8,128)S(1)} %collective-permute-done.3.refs_6_), channel_id=1, source_target_pairs={{0,4},{4,0},{8,12},{12,8},{1,5},{5,1},{9,13},{13,9},{2,6},{6,2},{1... | collective-permute-start | bytes 196616 | tf_op jit(solution)/shard_map/ppermute | solution.py:201
  13.7 3.1 %collective-permute-start.8 = (f32[2,2,4,512]{3,2,1,0:T(4,128)S(1)}, f32[2,2,4,512]{3,2,1,0:T(4,128)S(1)}, u32[]{:S(2)}, u32[]{:S(2)}) collective-permute-start(f32[2,2,4,512]{3,2,1,0:T(4,128)S(1)} %slice_select_fusion.3), channel_id=1, source_target_pairs={{0,1},{1,0},{2,3},{3,2},{4,5},{5,4},{6,7},{7,6},{8,9},{9,8},{10,11... | collective-permute-start | bytes 98312 | tf_op jit(solution)/shard_map/ppermute | solution.py:189
